TPU v7x, 512 devices: a whole 4x4x16 slice. The times are simulated.
512 devices in a mesh: col: 8 (over z_hi, x), row: 64 (over z_lo, y, core).
Axes of the slice: x: 4, y: 4, z: 16 (z_hi: 2, z_lo: 8; z = z_hi * 8 + z_lo), core: 2. Of those that a mesh axis runs over, the one named last changes fastest.
Arguments:
- matrix: float32 [65536, 2048], P('row', 'col'), may hold values from -130 to 130
- keep: int32 [8, 256], P('col'), may hold values from 0 to 255, as said below
Outputs:
- rotated: float32 [65536, 2048], P('row', 'col')
- col_norms: float32 [2048], P('col')
Inputs may be any that keep to these rules, and one draw needn't show every extreme that they name: `keep`: each row is a permutation of 0 .. 255.
All inputs are finite; a program needn't handle non-finite values.
Results may differ from a plain program's by a relative error of at most 0.00022.
Values sent between devices are 32-bit elements; how exact they have to be, the bound alone decides.
No kernel may reach another device: no remote copies, remote signals or barrier semaphores. Data moves between devices by JAX's collectives and lax.ppermute only.
A program may use at most 64 MiB of HBM per device.

v0:
```python
import jax
import jax.numpy as jnp
from jax import lax
from jax.sharding import PartitionSpec as P

SWEEPS = 4


STEP_GAIN = 3.0
EPSILON = 1e-06


def from_behind(shard, axis, by):
    peers = lax.axis_size(axis)
    return lax.ppermute(shard, axis, [(i, (i + by) % peers) for i in range(peers)])


def product(left, right):
    return jnp.dot(left, right, precision=lax.Precision.HIGHEST, preferred_element_type=jnp.float32)


def inner_gram(left, right):
    return lax.dot_general(
        left,
        right,
        (((0,), (0,)), ((), ())),
        precision=lax.Precision.HIGHEST,
        preferred_element_type=jnp.float32,
    )


def sweeps(gram):
    width = gram.shape[0]
    scale = jnp.trace(gram) / width
    scaled = gram / scale
    ladder = (jnp.arange(width, dtype=jnp.float32) - (width - 1) / 2.0) / width
    ident = jnp.eye(width, dtype=jnp.float32)
    basis = ident
    for sweep in range(SWEEPS):
        skew = STEP_GAIN / width * (scaled * ladder[None, :] - ladder[:, None] * scaled)
        turn = ident + skew + 0.5 * product(skew, skew)
        scaled = inner_gram(turn, product(scaled, turn))
        basis = product(basis, turn)
    return (basis, scaled * scale)


def shards(matrix, keep):
    width = matrix.shape[1]
    half = width // 2
    gram = lax.psum(inner_gram(matrix, matrix), "row")
    basis, moved = sweeps(gram)
    first = product(matrix, basis)
    order = keep[0]
    selector = (jnp.arange(width, dtype=jnp.int32)[:, None] == order[None, :]).astype(jnp.float32)
    reordered = product(first, selector)
    kept = reordered[:, :half]
    given = reordered[:, half:]
    arrived = from_behind(given, "col", 1)
    paired = jnp.concatenate([kept, arrived], axis=1)
    gram_two = lax.psum(inner_gram(paired, paired), "row")
    basis_two, moved_two = sweeps(gram_two)
    rotated = product(paired, basis_two)
    total_rows = rotated.shape[0] * lax.axis_size("row")
    squares = lax.psum(jnp.sum(rotated * rotated, axis=0), "row")
    col_norms = jnp.sqrt(squares / total_rows + EPSILON)
    return (rotated, col_norms)


def solution(mesh):
    return jax.shard_map(
        shards,
        mesh=mesh,
        in_specs=(P("row", "col"), P("col", None)),
        out_specs=(P("row", "col"), P("col")),
        check_vma=False,
    )
```

profile of v0, /device:TPU:1, one launch (start us, length us, event | category | flops | bytes accessed | tf_op | source)
XLA Modules:
  0.0 1846.0 jit_solution(7098216067841335403)
XLA Ops:
  7.2 0.0 copy-start
  7.2 0.0 all-reduce.3.cloned.1.call-start
  7.2 1.2 copy-done
  8.4 2.5 fusion.83
  10.9 0.0 all-reduce.3.cloned.1.call-update
  11.0 0.0 all-reduce.5.cloned.1.call-start
  11.0 788.0 %all-reduce.3.cloned.1.call-done = f32[256,256]{1,0:T(8,128)} async-done(((f32[256,256]{1,0:T(8,128)}), f32[256,256]{1,0:T(8,128)}) %all-reduce.3.cloned.1.call-update) | async-done | bytes 262160 | tf_op jit(solution)/shard_map/psum | solution.py:50
  799.0 0.0 copy-start.1
  799.0 1.7 select_reduce_fusion.1
  801.3 0.0 copy-done.1
  801.3 0.5 fusion.7
  801.8 0.3 fusion.43
  802.1 0.4 fusion.70
  802.5 0.6 fusion.84
  803.1 0.5 fusion.6
  803.6 0.4 fusion.86
  804.0 0.6 fusion.87
  804.6 0.4 fusion.85
  805.0 0.5 fusion.5
  805.5 0.4 fusion.89
  805.9 0.6 fusion.90
  806.5 0.4 fusion.88
  806.9 0.5 fusion.4
  807.3 0.4 fusion.91
  807.7 1.9 fusion.92
  809.6 0.0 copy-start.3
  809.6 0.7 copy-done.3
  810.3 0.7 fusion.44
  811.0 0.1 fusion.82
  811.1 3.3 collective-permute-start
  814.4 19.8 %collective-permute-done = f32[1024,128]{0,1:T(8,128)S(1)} collective-permute-done((f32[1024,128]{0,1:T(8,128)S(1)}, f32[1024,128]{0,1:T(8,128)S(1)}, u32[]{:S(2)}, u32[]{:S(2)}) %collective-permute-start) | collective-permute-done | bytes 524320 | tf_op jit(solution)/shard_map/ppermute | solution.py:15
  834.2 1.7 fusion.9
  835.9 0.0 all-reduce.5.cloned.1.call-update
  835.9 778.4 %all-reduce.5.cloned.1.call-done = f32[256,256]{1,0:T(8,128)} async-done(((f32[256,256]{1,0:T(8,128)}), f32[256,256]{1,0:T(8,128)}) %all-reduce.5.cloned.1.call-update) | async-done | bytes 262160 | tf_op jit(solution)/shard_map/psum | solution.py:60
  1614.3 0.0 copy-start.2
  1614.3 1.7 select_reduce_fusion
  1616.6 0.0 copy-done.2
  1616.6 0.5 fusion.3
  1617.1 0.3 fusion.42
  1617.4 0.4 fusion.71
  1617.8 0.6 fusion.93
  1618.4 0.5 fusion.2
  1618.9 0.4 fusion.95
  1619.3 0.6 fusion.96
  1619.9 0.4 fusion.94
  1620.3 0.5 fusion.1
  1620.8 0.4 fusion.98
  1621.2 0.6 fusion.99
  1621.8 0.4 fusion.97
  1622.2 0.5 fusion
  1622.7 0.4 fusion.100
  1623.1 2.8 multiply_reduce_fusion
  1625.9 212.7 %psum.23 = f32[256]{0:T(256)S(1)} all-reduce(f32[256]{0:T(256)S(1)} %get-tuple-element.4), channel_id=1, replica_groups=mesh['col'=8,'row'=64] {'row'}, use_global_device_ids=true, to_apply=%region_5.6 | all-reduce | flops 256 | bytes 2048 | tf_op jit(solution)/shard_map/psum | solution.py:64
  1838.6 0.6 add_sqrt_fusion
  (1 shorter events, 0.0 us)
Async XLA Ops:
  7.2 1.2 copy-start
  7.2 791.8 %all-reduce.3.cloned.1.call-start = ((), (), s32[]{:S(2)}) async-start(), calls=%async_computation | async-start | bytes 524288 | tf_op jit(solution)/shard_map/psum | solution.py:50
  11.0 1603.4 %all-reduce.5.cloned.1.call-start = ((), (), s32[]{:S(2)}) async-start(), calls=%async_computation.1 | async-start | bytes 524288 | tf_op jit(solution)/shard_map/psum | solution.py:60
  799.0 2.3 copy-start.1
  809.6 0.7 copy-start.3
  811.1 23.1 %collective-permute-start = (f32[1024,128]{0,1:T(8,128)S(1)}, f32[1024,128]{0,1:T(8,128)S(1)}, u32[]{:S(2)}, u32[]{:S(2)}) collective-permute-start(f32[1024,128]{0,1:T(8,128)S(1)} %get-tuple-element.3), channel_id=1, source_target_pairs={{0,64},{64,128},{128,192},{192,256},{256,320},{320,384},{384,448},... | collective-permute-start | bytes 1572872 | tf_op jit(solution)/shard_map/ppermute | solution.py:15
  1614.3 2.3 copy-start.2
Sparse Core Ops, SparseCore 0:
  11.5 787.4 all-reduce.2
  836.1 778.2 all-reduce.4
where the time goes:
time: 1850 us
  waiting for transfers between devices  1590 us (86%)
  blocking collectives  213 us (12%)
  matrix products  22.2 us (1%)
    psum x1, waiting for transfers between devices, shards(): gram = lax.psum(inner_gram(matrix, matrix), 'row')  788 us
    psum x1, waiting for transfers between devices, shards(): gram_two = lax.psum(inner_gram(paired, paired), 'row')  778 us
    psum x1, blocking collectives, shards(): squares = lax.psum(jnp.sum(rotated * rotated, axis=0), 'row')  213 us
  transfers between devices with their start and end apart: 3, of which 3 were waited for; matrix products, arithmetic and copies ran while one was open for 0% of the time, Pallas kernels for 0%

commit v1 on v0

--- a/solution.py
+++ b/solution.py
@@ -1,13 +1,18 @@
 import jax
 import jax.numpy as jnp
 from jax import lax
-from jax.sharding import PartitionSpec as P
+from jax.sharding import Mesh, PartitionSpec as P
 
 SWEEPS = 4
 
 
 STEP_GAIN = 3.0
 EPSILON = 1e-06
+
+NEAR = ("y", "core")
+FAR = "z_lo"
+ROW = ("z_lo", "y", "core")
+COL = ("z_hi", "x")
 
 
 def from_behind(shard, axis, by):
@@ -29,6 +34,20 @@
     )
 
 
+def spread(piece, axis):
+    peers = lax.axis_size(axis)
+    copies = jnp.broadcast_to(piece[None], (peers,) + piece.shape)
+    return lax.all_to_all(copies, axis, 0, 0, tiled=True)
+
+
+def row_sum(part):
+    near = lax.axis_size(NEAR)
+    slices = part.reshape(near, part.shape[0] // near, part.shape[1])
+    mine = jnp.sum(lax.all_to_all(slices, NEAR, 0, 0, tiled=True), axis=0)
+    mine = jnp.sum(spread(mine, FAR), axis=0)
+    return spread(mine, NEAR).reshape(part.shape)
+
+
 def sweeps(gram):
     width = gram.shape[0]
     scale = jnp.trace(gram) / width
@@ -47,30 +66,31 @@
 def shards(matrix, keep):
     width = matrix.shape[1]
     half = width // 2
-    gram = lax.psum(inner_gram(matrix, matrix), "row")
+    gram = row_sum(inner_gram(matrix, matrix))
     basis, moved = sweeps(gram)
-    first = product(matrix, basis)
     order = keep[0]
     selector = (jnp.arange(width, dtype=jnp.int32)[:, None] == order[None, :]).astype(jnp.float32)
-    reordered = product(first, selector)
+    reordered = product(matrix, product(basis, selector))
     kept = reordered[:, :half]
-    given = reordered[:, half:]
-    arrived = from_behind(given, "col", 1)
-    paired = jnp.concatenate([kept, arrived], axis=1)
-    gram_two = lax.psum(inner_gram(paired, paired), "row")
+    moved = inner_gram(selector, product(moved, selector))
+    arrived = from_behind(reordered[:, half:], COL, 1)
+    arrived_gram = from_behind(moved[half:, half:], COL, 1)
+    cross = row_sum(inner_gram(kept, arrived))
+    gram_two = jnp.block([[moved[:half, :half], cross], [cross.T, arrived_gram]])
     basis_two, moved_two = sweeps(gram_two)
-    rotated = product(paired, basis_two)
-    total_rows = rotated.shape[0] * lax.axis_size("row")
-    squares = lax.psum(jnp.sum(rotated * rotated, axis=0), "row")
+    rotated = product(kept, basis_two[:half]) + product(arrived, basis_two[half:])
+    total_rows = rotated.shape[0] * lax.axis_size(ROW)
+    squares = jnp.maximum(jnp.diagonal(moved_two), 0.0)
     col_norms = jnp.sqrt(squares / total_rows + EPSILON)
     return (rotated, col_norms)
 
 
 def solution(mesh):
+    fine = Mesh(mesh.devices.reshape(2, 4, 8, 4, 2), ("z_hi", "x", "z_lo", "y", "core"))
     return jax.shard_map(
         shards,
-        mesh=mesh,
-        in_specs=(P("row", "col"), P("col", None)),
-        out_specs=(P("row", "col"), P("col")),
+        mesh=fine,
+        in_specs=(P(ROW, COL), P(COL, None)),
+        out_specs=(P(ROW, COL), P(COL)),
         check_vma=False,
     )

time: 1850 us -> 176 us (0.10)
  waiting for transfers between devices: 1590 us -> 71.3 us
  blocking collectives: 213 us -> 36.2 us
  starting transfers between devices: 3.36 us -> 33.8 us
    psum x2 -> x0, waiting for transfers between devices: 1570 us -> none  [the longest x1 788 us: shards(): gram = lax.psum(inner_gram(matrix, matrix), 'row')]
    psum x1 -> x0, blocking collectives: 213 us -> none  [shards(): squares = lax.psum(jnp.sum(rotated * rotated, axis=0), 'row')]
    all_to_all x0 -> x2, blocking collectives: none -> 36.2 us  [the longest x1 20.4 us: spread(): return lax.all_to_all(copies, axis, 0, 0, tiled=True)]
    all_to_all x0 -> x4, starting transfers between devices: none -> 28.6 us  [the longest x3 23.9 us: spread(): return lax.all_to_all(copies, axis, 0, 0, tiled=True)]
    ppermute x1 -> x2, waiting for transfers between devices: 19.8 us -> 48 us  [from_behind(): lax.ppermute(shard, axis, [(i, (i + by) % peers) for i in range(peers)])]
    all_to_all x0 -> x4, waiting for transfers between devices: none -> 23.3 us  [the longest x3 18.7 us: spread(): return lax.all_to_all(copies, axis, 0, 0, tiled=True)]
  transfers between devices with their start and end apart: 3 -> 6, of which waited for: 3 -> 5; matrix products, arithmetic and copies ran while one was open for 0% -> 1% of each run, Pallas kernels for 0% -> 0%
where the time goes in v1:
time: 176 us
  waiting for transfers between devices  71.3 us (41%)
  blocking collectives  36.2 us (21%)
  starting transfers between devices  33.8 us (19%)
  matrix products  23.4 us (13%)
  local copies, waits for them, and re-layouts  6.38 us (4%)
  between operations  2.37 us (1%)
  other arithmetic  2.14 us (1%)
    ppermute x2, waiting for transfers between devices, from_behind(): lax.ppermute(shard, axis, [(i, (i + by) % peers) for i in range(peers)])  48 us
    all_to_all x3, starting transfers between devices, spread(): return lax.all_to_all(copies, axis, 0, 0, tiled=True)  23.9 us
    all_to_all x1, blocking collectives, spread(): return lax.all_to_all(copies, axis, 0, 0, tiled=True)  20.4 us
    all_to_all x3, waiting for transfers between devices, spread(): return lax.all_to_all(copies, axis, 0, 0, tiled=True)  18.7 us
    all_to_all x1, blocking collectives, row_sum(): mine = jnp.sum(lax.all_to_all(slices, NEAR, 0, 0, tiled=True), axis=0)  15.8 us
    dot_general x29, matrix products, product(): jnp.dot(left, right, precision=lax.Precision.HIGHEST, preferred_element_t...  15.1 us
    dot_general x11, matrix products, inner_gram(): lax.dot_general(left, right, (((0,), (0,)), ((), ())), precision=lax.Prec...  8.22 us
    ppermute x2, starting transfers between devices, from_behind(): lax.ppermute(shard, axis, [(i, (i + by) % peers) for i in range(peers)])  5.22 us
  transfers between devices with their start and end apart: 6, of which 5 were waited for; matrix products, arithmetic and copies ran while one was open for 1% of the time, Pallas kernels for 0%

profile of v1, /device:TPU:1, one launch (start us, length us, event | category | flops | bytes accessed | tf_op | source)
XLA Modules:
  0.0 175.5 jit_solution(18189518004641508600)
XLA Ops:
  0.6 1.2 copy-done
  1.9 1.8 %fusion.83 = f32[256,256]{1,0:T(8,128)S(1)} fusion(f32[1024,256]{1,0:T(8,128)S(1)} %copy-done), kind=kOutput, calls=%fused_computation.115 | convolution fusion | flops 805306368 | bytes 1310720 | tf_op jit(solution)/shard_map/dot_general | solution.py:28
  3.7 15.8 %all_to_all.30 = f32[8,32,256]{2,1,0:T(8,128)S(1)} all-to-all(f32[8,32,256]{2,1,0:T(8,128)S(1)} %bitcast.70), channel_id=1, replica_groups=mesh['z_hi'=2,'x'=4,'z_lo'=8,'y'=4,'core'=2] {'y','core'}, dimensions={0} | all-to-all | bytes 524288 | tf_op jit(solution)/shard_map/all_to_all | solution.py:46
  19.5 20.4 %all_to_all.31 = f32[8,32,256]{2,1,0:T(8,128)S(1)} all-to-all(f32[8,32,256]{2,1,0:T(8,128)S(1)} %broadcast_in_dim.17), channel_id=1, replica_groups=mesh['z_hi'=2,'x'=4,'z_lo'=8,'y'=4,'core'=2] {'z_lo'}, dimensions={0} | all-to-all | bytes 524288 | tf_op jit(solution)/shard_map/all_to_all | solution.py:40
  39.9 0.7 broadcast_in_dim.18
  40.7 9.1 %all-to-all-start.2 = ((f32[8,32,256]{2,1,0:T(8,128)}), f32[8,32,256]{2,1,0:T(8,128)S(1)}, u32[]{:S(2)}, u32[]{:S(2)}) async-start(f32[8,32,256]{2,1,0:T(8,128)} %broadcast_in_dim.18), calls=%async_computation.2 | async-start | bytes 524288 | tf_op jit(solution)/shard_map/all_to_all | solution.py:40
  49.8 6.5 %all-to-all-done.2 = f32[8,32,256]{2,1,0:T(8,128)S(1)} async-done(((f32[8,32,256]{2,1,0:T(8,128)}), f32[8,32,256]{2,1,0:T(8,128)S(1)}, u32[]{:S(2)}, u32[]{:S(2)}) %all-to-all-start.2) | async-done | bytes 262176 | tf_op jit(solution)/shard_map/all_to_all | solution.py:40
  56.3 0.7 select_reduce_fusion.1
  57.7 0.1 subtract_multiply_fusion
  57.8 0.4 fusion.7
  58.2 0.4 fusion.84
  58.6 0.3 fusion.44
  58.9 0.6 fusion.85
  59.5 0.5 fusion.6
  60.0 0.4 fusion.87
  60.4 0.6 fusion.88
  61.0 0.5 fusion.5
  61.4 0.4 fusion.90
  61.8 0.6 fusion.91
  62.4 0.5 fusion.4
  62.9 0.4 fusion.86
  63.3 0.4 fusion.89
  63.7 0.4 fusion.92
  64.1 0.7 copy-done.3
  64.8 0.3 fusion.30
  65.1 1.9 %convolution_bitcast_fusion = f32[1024,256]{0,1:T(8,128)S(1)} fusion(f32[256,256]{1,0:T(8,128)S(1)} %fusion.30, f32[1024,256]{1,0:T(8,128)S(1)} %copy-done), kind=kOutput, calls=%fused_computation.2 | convolution fusion | flops 805306368 | bytes 2359296 | tf_op jit(solution)/shard_map/dot_general | solution.py:24
  67.0 3.3 %collective-permute-start = (f32[1024,128]{0,1:T(8,128)S(1)}, f32[1024,128]{0,1:T(8,128)S(1)}, u32[]{:S(2)}, u32[]{:S(2)}) collective-permute-start(f32[1024,128]{0,1:T(8,128)S(1)} %slice.28), channel_id=1, source_target_pairs={{0,64},{64,128},{128,192},{192,256},{256,320},{320,384},{384,448},... | collective-permute-start | bytes 1572872 | tf_op jit(solution)/shard_map/ppermute | solution.py:20
  70.3 0.4 fusion.93
  70.7 0.6 convolution_multiply_fusion.5
  71.3 48.0 %collective-permute-done = f32[1024,128]{0,1:T(8,128)S(1)} collective-permute-done((f32[1024,128]{0,1:T(8,128)S(1)}, f32[1024,128]{0,1:T(8,128)S(1)}, u32[]{:S(2)}, u32[]{:S(2)}) %collective-permute-start) | collective-permute-done | bytes 524320 | tf_op jit(solution)/shard_map/ppermute | solution.py:20
  119.3 1.2 fusion.10
  120.5 4.7 %all-to-all-start.3 = ((f32[8,16,128]{2,1,0:T(8,128)}), f32[8,16,128]{2,1,0:T(8,128)S(1)}, u32[]{:S(2)}, u32[]{:S(2)}) async-start(f32[8,16,128]{2,1,0:T(8,128)} %bitcast.5), calls=%async_computation.3 | async-start | bytes 131072 | tf_op jit(solution)/shard_map/all_to_all | solution.py:46
  125.2 0.3 fusion.29
  125.5 4.6 %all-to-all-done.3 = f32[8,16,128]{2,1,0:T(8,128)S(1)} async-done(((f32[8,16,128]{2,1,0:T(8,128)}), f32[8,16,128]{2,1,0:T(8,128)S(1)}, u32[]{:S(2)}, u32[]{:S(2)}) %all-to-all-start.3) | async-done | bytes 65568 | tf_op jit(solution)/shard_map/all_to_all | solution.py:46
  130.0 0.6 broadcast_in_dim.20
  130.7 9.3 %all-to-all-start.4 = ((f32[8,16,128]{2,1,0:T(8,128)}), f32[8,16,128]{2,1,0:T(8,128)S(1)}, u32[]{:S(2)}, u32[]{:S(2)}) async-start(f32[8,16,128]{2,1,0:T(8,128)} %broadcast_in_dim.20), calls=%async_computation.4 | async-start | bytes 131072 | tf_op jit(solution)/shard_map/all_to_all | solution.py:40
  140.0 0.4 fusion.28
  140.4 1.9 %collective-permute-start.1 = (f32[128,128]{1,0:T(8,128)S(1)}, f32[128,128]{1,0:T(8,128)S(1)}, u32[]{:S(2)}, u32[]{:S(2)}) collective-permute-start(f32[128,128]{1,0:T(8,128)S(1)} %get-tuple-element.5), channel_id=1, source_target_pairs={{0,64},{64,128},{128,192},{192,256},{256,320},{320,384},{384,448},... | collective-permute-start | bytes 196616 | tf_op jit(solution)/shard_map/ppermute | solution.py:20
  142.4 7.4 %all-to-all-done.4 = f32[8,16,128]{2,1,0:T(8,128)S(1)} async-done(((f32[8,16,128]{2,1,0:T(8,128)}), f32[8,16,128]{2,1,0:T(8,128)S(1)}, u32[]{:S(2)}, u32[]{:S(2)}) %all-to-all-start.4) | async-done | bytes 65568 | tf_op jit(solution)/shard_map/all_to_all | solution.py:40
  149.8 0.6 broadcast_in_dim.21
  150.4 5.5 %all-to-all-start.5 = ((f32[8,16,128]{2,1,0:T(8,128)}), f32[8,16,128]{2,1,0:T(8,128)S(1)}, u32[]{:S(2)}, u32[]{:S(2)}) async-start(f32[8,16,128]{2,1,0:T(8,128)} %broadcast_in_dim.21), calls=%async_computation.5 | async-start | bytes 131072 | tf_op jit(solution)/shard_map/all_to_all | solution.py:40
  155.9 4.9 %all-to-all-done.5 = f32[8,16,128]{2,1,0:T(8,128)S(1)} async-done(((f32[8,16,128]{2,1,0:T(8,128)}), f32[8,16,128]{2,1,0:T(8,128)S(1)}, u32[]{:S(2)}, u32[]{:S(2)}) %all-to-all-start.5) | async-done | bytes 65568 | tf_op jit(solution)/shard_map/all_to_all | solution.py:40
  160.7 0.1 copy.10
  160.8 0.6 select_reduce_fusion
  162.1 0.5 fusion.3
  162.6 0.3 fusion.43
  162.9 0.4 fusion.80
  163.3 0.6 fusion.94
  163.9 0.5 fusion.2
  164.4 0.4 fusion.96
  164.8 0.6 fusion.97
  165.4 0.5 fusion.1
  165.9 0.4 fusion.99
  166.3 0.6 fusion.100
  166.9 0.5 fusion
  167.4 0.4 fusion.102
  167.8 0.6 convolution_multiply_fusion
  168.4 2.3 %gather_fusion = f32[256]{0:T(256)S(1)} fusion(f32[256,256]{1,0:T(8,128)S(1)} %convolution_multiply_fusion, s32[256]{0:T(256)S(1)} %bitcast.66), kind=kCustom, calls=%fused_computation | custom fusion | bytes 4096 | tf_op jit(solution)/shard_map/jit(diagonal)/cond/branch_0_fun/gather | solution.py:83
  170.7 0.6 add_sqrt_fusion
  171.3 0.4 fusion.95
  171.7 0.4 fusion.98
  172.1 0.4 fusion.101
  172.5 1.0 fusion.8
  173.5 2.0 %convolution_add_fusion = f32[1024,256]{1,0:T(8,128)} fusion(f32[1024,256]{1,0:T(8,128)S(1)} %fusion.8, f32[1024,128]{0,1:T(8,128)S(1)} %copy-done.2, f32[256,256]{1,0:T(8,128)S(1)} %fusion.101), kind=kOutput, calls=%fused_computation.1 | convolution fusion | flops 402915328 | bytes 2752512 | tf_op jit(solution)/shard_map/dot_general | solution.py:24
  (18 shorter events, 0.2 us)
Async XLA Ops:
  0.6 1.2 copy-start
  40.7 15.6 %all-to-all-start.2 = ((f32[8,32,256]{2,1,0:T(8,128)}), f32[8,32,256]{2,1,0:T(8,128)S(1)}, u32[]{:S(2)}, u32[]{:S(2)}) async-start(f32[8,32,256]{2,1,0:T(8,128)} %broadcast_in_dim.18), calls=%async_computation.2 | async-start | bytes 524288 | tf_op jit(solution)/shard_map/all_to_all | solution.py:40
  64.1 0.7 copy-start.3
  67.0 52.3 %collective-permute-start = (f32[1024,128]{0,1:T(8,128)S(1)}, f32[1024,128]{0,1:T(8,128)S(1)}, u32[]{:S(2)}, u32[]{:S(2)}) collective-permute-start(f32[1024,128]{0,1:T(8,128)S(1)} %slice.28), channel_id=1, source_target_pairs={{0,64},{64,128},{128,192},{192,256},{256,320},{320,384},{384,448},... | collective-permute-start | bytes 1572872 | tf_op jit(solution)/shard_map/ppermute | solution.py:20
  119.3 1.2 copy-start.1
  120.5 9.6 %all-to-all-start.3 = ((f32[8,16,128]{2,1,0:T(8,128)}), f32[8,16,128]{2,1,0:T(8,128)S(1)}, u32[]{:S(2)}, u32[]{:S(2)}) async-start(f32[8,16,128]{2,1,0:T(8,128)} %bitcast.5), calls=%async_computation.3 | async-start | bytes 131072 | tf_op jit(solution)/shard_map/all_to_all | solution.py:46
  130.7 19.1 %all-to-all-start.4 = ((f32[8,16,128]{2,1,0:T(8,128)}), f32[8,16,128]{2,1,0:T(8,128)S(1)}, u32[]{:S(2)}, u32[]{:S(2)}) async-start(f32[8,16,128]{2,1,0:T(8,128)} %broadcast_in_dim.20), calls=%async_computation.4 | async-start | bytes 131072 | tf_op jit(solution)/shard_map/all_to_all | solution.py:40
  140.4 20.4 %collective-permute-start.1 = (f32[128,128]{1,0:T(8,128)S(1)}, f32[128,128]{1,0:T(8,128)S(1)}, u32[]{:S(2)}, u32[]{:S(2)}) collective-permute-start(f32[128,128]{1,0:T(8,128)S(1)} %get-tuple-element.5), channel_id=1, source_target_pairs={{0,64},{64,128},{128,192},{192,256},{256,320},{320,384},{384,448},... | collective-permute-start | bytes 196616 | tf_op jit(solution)/shard_map/ppermute | solution.py:20
  150.4 10.3 %all-to-all-start.5 = ((f32[8,16,128]{2,1,0:T(8,128)}), f32[8,16,128]{2,1,0:T(8,128)S(1)}, u32[]{:S(2)}, u32[]{:S(2)}) async-start(f32[8,16,128]{2,1,0:T(8,128)} %broadcast_in_dim.21), calls=%async_computation.5 | async-start | bytes 131072 | tf_op jit(solution)/shard_map/all_to_all | solution.py:40
  172.5 1.1 copy-start.2

commit v2 on v1

--- a/solution.py
+++ b/solution.py
@@ -1,3 +1,5 @@
+import functools
+
 import jax
 import jax.numpy as jnp
 from jax import lax
@@ -15,9 +17,19 @@
 COL = ("z_hi", "x")
 
 
-def from_behind(shard, axis, by):
-    peers = lax.axis_size(axis)
-    return lax.ppermute(shard, axis, [(i, (i + by) % peers) for i in range(peers)])
+DIRECT, RING, TWO, ONE = 304, 240, 240, 240
+
+
+def send(shard, pairs):
+    return lax.ppermute(shard, COL, pairs)
+
+
+def inside(source, target):
+    return [(source, target), (4 + source, 4 + target)]
+
+
+def across(source, target):
+    return [(source, 4 + target), (4 + source, target)]
 
 
 def product(left, right):
@@ -40,12 +52,14 @@
     return lax.all_to_all(copies, axis, 0, 0, tiled=True)
 
 
-def row_sum(part):
+def near_sum(part):
     near = lax.axis_size(NEAR)
     slices = part.reshape(near, part.shape[0] // near, part.shape[1])
-    mine = jnp.sum(lax.all_to_all(slices, NEAR, 0, 0, tiled=True), axis=0)
-    mine = jnp.sum(spread(mine, FAR), axis=0)
-    return spread(mine, NEAR).reshape(part.shape)
+    return jnp.sum(lax.all_to_all(slices, NEAR, 0, 0, tiled=True), axis=0)
+
+
+def far_sum(piece):
+    return jnp.sum(spread(piece, FAR), axis=0)
 
 
 def sweeps(gram):
@@ -64,24 +78,72 @@
 
 
 def shards(matrix, keep):
-    width = matrix.shape[1]
+    rows, width = matrix.shape
     half = width // 2
-    gram = row_sum(inner_gram(matrix, matrix))
-    basis, moved = sweeps(gram)
+    place = lax.axis_index("x")
     order = keep[0]
     selector = (jnp.arange(width, dtype=jnp.int32)[:, None] == order[None, :]).astype(jnp.float32)
-    reordered = product(matrix, product(basis, selector))
-    kept = reordered[:, :half]
-    moved = inner_gram(selector, product(moved, selector))
-    arrived = from_behind(reordered[:, half:], COL, 1)
-    arrived_gram = from_behind(moved[half:, half:], COL, 1)
-    cross = row_sum(inner_gram(kept, arrived))
-    gram_two = jnp.block([[moved[:half, :half], cross], [cross.T, arrived_gram]])
-    basis_two, moved_two = sweeps(gram_two)
-    rotated = product(kept, basis_two[:half]) + product(arrived, basis_two[half:])
-    total_rows = rotated.shape[0] * lax.axis_size(ROW)
-    squares = jnp.maximum(jnp.diagonal(moved_two), 0.0)
-    col_norms = jnp.sqrt(squares / total_rows + EPSILON)
+
+    direct, ring, two, one = jnp.split(matrix, [DIRECT, DIRECT + RING, DIRECT + RING + TWO])
+    turned = send(ring, sum([inside(i, (i + 1) % 4) for i in range(4)], []))
+    at_two = send(two, inside(3, 2))
+    at_one = send(one, inside(3, 1))
+    direct = send(direct, [(i, (i + 1) % 8) for i in range(8)])
+    slices = near_sum(inner_gram(matrix, matrix))
+    turned, at_two, at_one, slices = lax.optimization_barrier((turned, at_two, at_one, slices))
+    crossed_two = send(at_two, across(2, 0))
+    crossed_one = send(at_one, across(1, 0))
+    crossed_ring = send(turned, across(0, 0))
+    shifted = send(matrix[DIRECT + RING :], sum([inside(i, i + 1) for i in range(3)], []))
+
+    def turn_first(slices):
+        gram = spread(far_sum(slices), NEAR).reshape(width, width)
+        basis, moved = sweeps(gram)
+        reordered = product(basis, selector)
+        moved = inner_gram(selector, product(moved, selector))
+        given = jnp.concatenate([reordered[:, half:], moved[half:, half:]], axis=0)
+        share = given.shape[0] // lax.axis_size(NEAR)
+        mine = lax.dynamic_slice_in_dim(given, lax.axis_index(NEAR) * share, share, 0)
+        return (reordered[:, :half], moved[:half, :half], mine)
+
+    blank = functools.partial(jnp.zeros, dtype=jnp.float32)
+    kept_basis, kept_gram, mine = lax.cond(
+        order[0] >= 0,
+        turn_first,
+        lambda slices: (blank((width, half)), blank((half, half)), blank((48, half))),
+        slices,
+    )
+    mine = send(mine, [(i, (i + 1) % 8) for i in range(8)])
+
+    direct, turned, crossed_two, crossed_one, crossed_ring, shifted, kept_basis = lax.optimization_barrier(
+        (direct, turned, crossed_two, crossed_one, crossed_ring, shifted, kept_basis)
+    )
+    first = place == 0
+    behind = jnp.concatenate(
+        [
+            direct,
+            jnp.where(first, crossed_ring, turned),
+            jnp.where(first, crossed_two, shifted[:TWO]),
+            jnp.where(first, crossed_one, shifted[TWO:]),
+        ],
+        axis=0,
+    )
+    cross = near_sum(inner_gram(behind, matrix))
+    cross = far_sum(product(cross, kept_basis))
+    both = spread(jnp.concatenate([cross, mine], axis=0), NEAR)
+    cut = cross.shape[0]
+    cross = both[:, :cut].reshape(width, half)
+    given = both[:, cut:].reshape(width + half, half)
+    given_basis, given_gram = given[:width], given[width:]
+    cross = inner_gram(given_basis, cross)
+    gram_two = jnp.block([[kept_gram, cross.T], [cross, given_gram]])
+    basis_two, gram_three = sweeps(gram_two)
+    rotated = product(matrix, product(kept_basis, basis_two[:half])) + product(
+        behind, product(given_basis, basis_two[half:])
+    )
+    ident = jnp.eye(width, dtype=jnp.float32)
+    squares = jnp.maximum(jnp.sum(gram_three * ident, axis=0), 0.0)
+    col_norms = jnp.sqrt(squares / (rows * lax.axis_size(ROW)) + EPSILON)
     return (rotated, col_norms)
 
 

time: 176 us -> 170 us (0.966)
  waiting for transfers between devices: 71.3 us -> 31.2 us
  starting transfers between devices: 33.8 us -> 55 us
  blocking collectives: 36.2 us -> 42.1 us
  local copies, waits for them, and re-layouts: 6.38 us -> 9.28 us
    ppermute x2 -> x9, waiting for transfers between devices: 48 us -> 5.11 us  [send(): return lax.ppermute(shard, COL, pairs)]
    ppermute x2 -> x9, starting transfers between devices: 5.22 us -> 31.3 us  [send(): return lax.ppermute(shard, COL, pairs)]
    all_to_all x1, blocking collectives: 20.4 us -> 32.2 us  [spread(): return lax.all_to_all(copies, axis, 0, 0, tiled=True)]
    all_to_all x3, starting transfers between devices: 23.9 us -> 17.3 us  [spread(): return lax.all_to_all(copies, axis, 0, 0, tiled=True)]
    all_to_all x1, blocking collectives: 15.8 us -> 9.95 us  [near_sum(): return jnp.sum(lax.all_to_all(slices, NEAR, 0, 0, tiled=True), axis=0)]
    all_to_all x3, waiting for transfers between devices: 18.7 us -> 21.7 us  [spread(): return lax.all_to_all(copies, axis, 0, 0, tiled=True)]
    slice x2 -> x7, local copies, waits for them, and re-layouts: 0.05 us -> 2.5 us  [the longest x1 1.93 us: shards(): matrix[DIRECT + RING:]]
    gather x1 -> x0, local copies, waits for them, and re-layouts: 2.34 us -> none  [shards(): squares = jnp.maximum(jnp.diagonal(moved_two), 0.0)]
  transfers between devices with their start and end apart: 6 -> 13, of which waited for: 5 -> 5; matrix products, arithmetic and copies ran while one was open for 1% -> 9% of each run, Pallas kernels for 0% -> 0%
where the time goes in v2:
time: 170 us; the launch traced here: 169 us
  starting transfers between devices  55 us (32%)
  blocking collectives  42.1 us (25%)
  waiting for transfers between devices  31.2 us (18%)
  matrix products  24.4 us (14%)
  local copies, waits for them, and re-layouts  9.28 us (5%)
  other arithmetic  3.54 us (2%)
  between operations  2.36 us (1%)
    all_to_all x1, blocking collectives, spread(): return lax.all_to_all(copies, axis, 0, 0, tiled=True)  32.2 us
    ppermute x9, starting transfers between devices, send(): return lax.ppermute(shard, COL, pairs)  31.3 us
    all_to_all x3, waiting for transfers between devices, spread(): return lax.all_to_all(copies, axis, 0, 0, tiled=True)  21.7 us
    all_to_all x3, starting transfers between devices, spread(): return lax.all_to_all(copies, axis, 0, 0, tiled=True)  17.3 us
    dot_general x31, matrix products, product(): jnp.dot(left, right, precision=lax.Precision.HIGHEST, preferred_element_t...  14.3 us
    dot_general x12, matrix products, inner_gram(): lax.dot_general(left, right, (((0,), (0,)), ((), ())), precision=lax.Prec...  10.1 us
    all_to_all x1, blocking collectives, near_sum(): return jnp.sum(lax.all_to_all(slices, NEAR, 0, 0, tiled=True), axis=0)  9.95 us
    all_to_all x1, starting transfers between devices, near_sum(): return jnp.sum(lax.all_to_all(slices, NEAR, 0, 0, tiled=True), axis=0)  6.42 us
  transfers between devices with their start and end apart: 13, of which 5 were waited for; matrix products, arithmetic and copies ran while one was open for 9% of the time, Pallas kernels for 0%

profile of v2, /device:TPU:1, one launch (start us, length us, event | category | flops | bytes accessed | tf_op | source)
XLA Modules:
  0.0 169.0 jit_solution(12790467916284397324)
XLA Ops:
  0.6 1.9 %slice.43 = f32[480,256]{1,0:T(8,128)} slice(f32[1024,256]{1,0:T(8,128)} %param.4), slice={[544:1024], [0:256]} | slice | bytes 983040 | tf_op jit(solution)/shard_map/slice | solution.py:97
  2.6 4.0 %collective-permute-start.7 = (f32[480,256]{1,0:T(8,128)}, f32[480,256]{1,0:T(8,128)S(1)}, u32[]{:S(2)}, u32[]{:S(2)}) collective-permute-start(f32[480,256]{1,0:T(8,128)} %slice.43), channel_id=1, source_target_pairs={{0,64},{256,320},{64,128},{320,384},{128,192},{384,448},{1,65},{25... | collective-permute-start | bytes 1474568 | tf_op jit(solution)/shard_map/ppermute | solution.py:24
  6.5 1.2 fusion.88
  7.8 1.4 collective-permute-start.3
  9.1 1.3 collective-permute-start.2
  10.5 3.0 %collective-permute-start.1 = (f32[240,256]{1,0:T(8,128)S(1)}, f32[240,256]{1,0:T(8,128)}, u32[]{:S(2)}, u32[]{:S(2)}) collective-permute-start(f32[240,256]{1,0:T(8,128)S(1)} %get-tuple-element.48), channel_id=1, source_target_pairs={{0,64},{256,320},{64,128},{320,384},{128,192},{384,448},{192,0},{4... | collective-permute-start | bytes 737288 | tf_op jit(solution)/shard_map/ppermute | solution.py:24
  13.5 2.5 %fusion.101 = f32[256,256]{1,0:T(8,128)} fusion(f32[1024,256]{1,0:T(8,128)S(1)} %copy-done), kind=kOutput, calls=%fused_computation.140 | convolution fusion | flops 805306368 | bytes 1310720 | tf_op jit(solution)/shard_map/dot_general | solution.py:40
  16.1 6.4 %all-to-all-start.2 = ((f32[8,32,256]{2,1,0:T(8,128)}), f32[8,32,256]{2,1,0:T(8,128)S(1)}, u32[]{:S(2)}, u32[]{:S(2)}) async-start(f32[8,32,256]{2,1,0:T(8,128)} %bitcast.3), calls=%async_computation.2 | async-start | bytes 524288 | tf_op jit(solution)/shard_map/all_to_all | solution.py:58
  22.5 2.1 %collective-permute-start = (f32[304,256]{1,0:T(8,128)S(1)}, f32[304,256]{1,0:T(8,128)S(1)}, u32[]{:S(2)}, u32[]{:S(2)}) collective-permute-start(f32[304,256]{1,0:T(8,128)S(1)} %split.12), channel_id=1, source_target_pairs={{0,64},{64,128},{128,192},{192,256},{256,320},{320,384},{384,448},... | collective-permute-start | bytes 933896 | tf_op jit(solution)/shard_map/ppermute | solution.py:24
  24.6 4.4 %all-to-all-done.2 = f32[8,32,256]{2,1,0:T(8,128)S(1)} async-done(((f32[8,32,256]{2,1,0:T(8,128)}), f32[8,32,256]{2,1,0:T(8,128)S(1)}, u32[]{:S(2)}, u32[]{:S(2)}) %all-to-all-start.2) | async-done | bytes 262176 | tf_op jit(solution)/shard_map/all_to_all | solution.py:58
  29.1 1.3 collective-permute-start.4
  30.4 1.3 collective-permute-start.5
  31.7 14.7 %collective-permute-start.6 = (f32[240,256]{1,0:T(8,128)}, f32[240,256]{1,0:T(8,128)}, u32[]{:S(2)}, u32[]{:S(2)}) collective-permute-start(f32[240,256]{1,0:T(8,128)} %collective-permute-done.1), channel_id=1, source_target_pairs={{0,256},{256,0},{1,257},{257,1},{2,258},{258,2},{3,259},{259,3},{4... | collective-permute-start | bytes 737288 | tf_op jit(solution)/shard_map/ppermute | solution.py:24
  46.4 0.7 copy-done.5
  47.1 0.5 slice.44
  48.3 53.8 %conditional.1 = (f32[256,128]{1,0:T(8,128)S(1)}, f32[128,128]{1,0:T(8,128)S(1)}, f32[48,128]{1,0:T(8,128)S(1)}) conditional(s32[]{:T(128)} %bitcast.4, () %tuple.19, (f32[32,256]{1,0:T(8,128)S(1)}, f32[256,256]{1,0:T(8,128)S(1)}) %tuple.20), branch_computations={%region_1.0_spmd, %region_2.5_spmd} | conditional | flops 3829071872 | bytes 18155728 | solution.py:110
  48.3 32.2 %all_to_all.28 = f32[8,32,256]{2,1,0:T(8,128)S(1)} all-to-all(f32[8,32,256]{2,1,0:T(8,128)S(1)} %broadcast_in_dim.6), channel_id=1, replica_groups=mesh['z_hi'=2,'x'=4,'z_lo'=8,'y'=4,'core'=2] {'z_lo'}, dimensions={0} | all-to-all | bytes 524288 | tf_op jit(solution)/shard_map/cond/branch_1_fun/all_to_all | solution.py:52
  80.6 0.7 broadcast_in_dim.7
  81.3 3.8 %all-to-all-start.1 = ((f32[8,32,256]{2,1,0:T(8,128)}), f32[8,32,256]{2,1,0:T(8,128)S(1)}, u32[]{:S(2)}, u32[]{:S(2)}) async-start(f32[8,32,256]{2,1,0:T(8,128)} %broadcast_in_dim.7), calls=%async_computation.1 | async-start | bytes 524288 | tf_op jit(solution)/shard_map/cond/branch_1_fun/all_to_all | solution.py:52
  85.1 6.5 %all-to-all-done.1 = f32[8,32,256]{2,1,0:T(8,128)S(1)} async-done(((f32[8,32,256]{2,1,0:T(8,128)}), f32[8,32,256]{2,1,0:T(8,128)S(1)}, u32[]{:S(2)}, u32[]{:S(2)}) %all-to-all-start.1) | async-done | bytes 262176 | tf_op jit(solution)/shard_map/cond/branch_1_fun/all_to_all | solution.py:52
  91.6 0.8 select_reduce_fusion
  93.1 0.4 fusion.3
  93.5 0.4 fusion.89
  94.2 0.6 fusion.90
  94.8 0.5 fusion.2
  95.7 0.6 fusion.93
  96.7 0.5 fusion.1
  97.2 0.4 fusion.95
  97.6 0.6 fusion.96
  98.2 0.4 fusion.94
  98.6 0.5 fusion
  99.1 0.4 fusion.99
  99.4 0.6 convolution_multiply_fusion
  100.1 0.4 fusion.97
  100.4 0.4 fusion.98
  101.2 0.6 convolution_bitcast_fusion
  102.2 0.5 copy-done.1
  102.7 1.3 slice_select_fusion.1
  104.0 1.8 %fusion.38 = f32[256,256]{1,0:T(8,128)S(1)} fusion(f32[1024,256]{1,0:T(8,128)S(1)} %copy-done, f32[240,256]{1,0:T(8,128)S(1)} %get-tuple-element.50, f32[240,256]{1,0:T(8,128)S(1)} %get-tuple-element.49, f32[240,256]{1,0:T(8,128)S(1)} %get-tuple-element.51, f32[304,256]{1,0:T(8,128)S(1)} %collective-permute-done), kind=kOutput, calls=%fused_computation.65 | convolution fusion | flops 806092800 | bytes 2359296 | tf_op jit(solution)/shard_map/dot_general | solution.py:40
  105.9 9.9 %all_to_all.29 = f32[8,32,256]{2,1,0:T(8,128)S(1)} all-to-all(f32[8,32,256]{2,1,0:T(8,128)S(1)} %bitcast.84), channel_id=1, replica_groups=mesh['z_hi'=2,'x'=4,'z_lo'=8,'y'=4,'core'=2] {'y','core'}, dimensions={0} | all-to-all | bytes 524288 | tf_op jit(solution)/shard_map/all_to_all | solution.py:58
  116.0 0.7 broadcast_in_dim.15
  116.7 7.4 %all-to-all-start.4 = ((f32[8,32,128]{2,1,0:T(8,128)}), f32[8,32,128]{2,1,0:T(8,128)S(1)}, u32[]{:S(2)}, u32[]{:S(2)}) async-start(f32[8,32,128]{2,1,0:T(8,128)} %broadcast_in_dim.15), calls=%async_computation.4 | async-start | bytes 262144 | tf_op jit(solution)/shard_map/all_to_all | solution.py:52
  124.1 2.2 %collective-permute-start.8 = (f32[48,128]{1,0:T(8,128)S(1)}, f32[48,128]{1,0:T(8,128)S(1)}, u32[]{:S(2)}, u32[]{:S(2)}) collective-permute-start(f32[48,128]{1,0:T(8,128)S(1)} %copy-done.4), channel_id=1, source_target_pairs={{0,64},{64,128},{128,192},{192,256},{256,320},{320,384},{384,448},... | collective-permute-start | bytes 73736 | tf_op jit(solution)/shard_map/ppermute | solution.py:24
  126.3 8.1 %all-to-all-done.4 = f32[8,32,128]{2,1,0:T(8,128)S(1)} async-done(((f32[8,32,128]{2,1,0:T(8,128)}), f32[8,32,128]{2,1,0:T(8,128)S(1)}, u32[]{:S(2)}, u32[]{:S(2)}) %all-to-all-start.4) | async-done | bytes 131104 | tf_op jit(solution)/shard_map/all_to_all | solution.py:52
  134.4 5.1 %collective-permute-done.8 = f32[48,128]{1,0:T(8,128)S(1)} collective-permute-done((f32[48,128]{1,0:T(8,128)S(1)}, f32[48,128]{1,0:T(8,128)S(1)}, u32[]{:S(2)}, u32[]{:S(2)}) %collective-permute-start.8) | collective-permute-done | bytes 24608 | tf_op jit(solution)/shard_map/ppermute | solution.py:24
  139.5 0.7 broadcast_in_dim.16
  140.2 6.1 %all-to-all-start.5 = ((f32[8,80,128]{2,1,0:T(8,128)}), f32[8,80,128]{2,1,0:T(8,128)S(1)}, u32[]{:S(2)}, u32[]{:S(2)}) async-start(f32[8,80,128]{2,1,0:T(8,128)} %broadcast_in_dim.16), calls=%async_computation.5 | async-start | bytes 655360 | tf_op jit(solution)/shard_map/all_to_all | solution.py:52
  146.3 7.1 %all-to-all-done.5 = f32[8,80,128]{2,1,0:T(8,128)S(1)} async-done(((f32[8,80,128]{2,1,0:T(8,128)}), f32[8,80,128]{2,1,0:T(8,128)S(1)}, u32[]{:S(2)}, u32[]{:S(2)}) %all-to-all-start.5) | async-done | bytes 327712 | tf_op jit(solution)/shard_map/all_to_all | solution.py:52
  153.5 0.4 fusion.75
  154.0 0.7 copy-done.2
  154.7 0.6 select_reduce_fusion.1
  156.0 0.5 fusion.35
  156.5 0.4 fusion.84
  157.2 0.6 fusion.103
  157.8 0.5 fusion.34
  158.7 0.6 fusion.106
  159.7 0.5 fusion.33
  160.6 0.6 fusion.109
  161.6 0.5 fusion.32
  163.6 0.6 fusion.36
  164.2 0.6 add_sqrt_fusion
  164.8 1.1 fusion.37
  165.9 1.9 %fusion.30 = f32[1024,256]{0,1:T(8,128)S(1)} fusion(f32[1024,256]{0,1:T(8,128)S(1)} %fusion.37, f32[256,256]{1,0:T(8,128)S(1)} %fusion.60, f32[1024,256]{1,0:T(8,128)S(1)} %copy-done), kind=kOutput, calls=%fused_computation.51 | convolution fusion | flops 805568512 | bytes 3407872 | tf_op jit(solution)/shard_map/dot_general | solution.py:36
  167.7 1.3 copy.9
  (51 shorter events, 5.4 us)
Async XLA Ops:
  0.6 12.9 %copy-start = (f32[1024,256]{1,0:T(8,128)S(1)}, f32[1024,256]{1,0:T(8,128)}, u32[]{:S(2)}) copy-start(f32[1024,256]{1,0:T(8,128)} %param.4) | copy-start | bytes 3145732
  2.6 99.6 %collective-permute-start.7 = (f32[480,256]{1,0:T(8,128)}, f32[480,256]{1,0:T(8,128)S(1)}, u32[]{:S(2)}, u32[]{:S(2)}) collective-permute-start(f32[480,256]{1,0:T(8,128)} %slice.43), channel_id=1, source_target_pairs={{0,64},{256,320},{64,128},{320,384},{128,192},{384,448},{1,65},{25... | collective-permute-start | bytes 1474568 | tf_op jit(solution)/shard_map/ppermute | solution.py:24
  7.8 21.3 %collective-permute-start.3 = (f32[240,256]{1,0:T(8,128)S(1)}, f32[240,256]{1,0:T(8,128)}, u32[]{:S(2)}, u32[]{:S(2)}) collective-permute-start(f32[240,256]{1,0:T(8,128)S(1)} %get-tuple-element.46), channel_id=1, source_target_pairs={{192,64},{448,320},{193,65},{449,321},{194,66},{450,322},{195,67},... | collective-permute-start | bytes 737288 | tf_op jit(solution)/shard_map/ppermute | solution.py:24
  9.1 19.9 %collective-permute-start.2 = (f32[240,256]{1,0:T(8,128)S(1)}, f32[240,256]{1,0:T(8,128)}, u32[]{:S(2)}, u32[]{:S(2)}) collective-permute-start(f32[240,256]{1,0:T(8,128)S(1)} %get-tuple-element.47), channel_id=1, source_target_pairs={{192,128},{448,384},{193,129},{449,385},{194,130},{450,386},{195,1... | collective-permute-start | bytes 737288 | tf_op jit(solution)/shard_map/ppermute | solution.py:24
  10.5 18.6 %collective-permute-start.1 = (f32[240,256]{1,0:T(8,128)S(1)}, f32[240,256]{1,0:T(8,128)}, u32[]{:S(2)}, u32[]{:S(2)}) collective-permute-start(f32[240,256]{1,0:T(8,128)S(1)} %get-tuple-element.48), channel_id=1, source_target_pairs={{0,64},{256,320},{64,128},{320,384},{128,192},{384,448},{192,0},{4... | collective-permute-start | bytes 737288 | tf_op jit(solution)/shard_map/ppermute | solution.py:24
  16.1 12.9 %all-to-all-start.2 = ((f32[8,32,256]{2,1,0:T(8,128)}), f32[8,32,256]{2,1,0:T(8,128)S(1)}, u32[]{:S(2)}, u32[]{:S(2)}) async-start(f32[8,32,256]{2,1,0:T(8,128)} %bitcast.3), calls=%async_computation.2 | async-start | bytes 524288 | tf_op jit(solution)/shard_map/all_to_all | solution.py:58
  22.5 79.6 %collective-permute-start = (f32[304,256]{1,0:T(8,128)S(1)}, f32[304,256]{1,0:T(8,128)S(1)}, u32[]{:S(2)}, u32[]{:S(2)}) collective-permute-start(f32[304,256]{1,0:T(8,128)S(1)} %split.12), channel_id=1, source_target_pairs={{0,64},{64,128},{128,192},{192,256},{256,320},{320,384},{384,448},... | collective-permute-start | bytes 933896 | tf_op jit(solution)/shard_map/ppermute | solution.py:24
  29.1 73.1 %collective-permute-start.4 = (f32[240,256]{1,0:T(8,128)}, f32[240,256]{1,0:T(8,128)}, u32[]{:S(2)}, u32[]{:S(2)}) collective-permute-start(f32[240,256]{1,0:T(8,128)} %collective-permute-done.2), channel_id=1, source_target_pairs={{128,256},{384,0},{129,257},{385,1},{130,258},{386,2},{131,259},{3... | collective-permute-start | bytes 737288 | tf_op jit(solution)/shard_map/ppermute | solution.py:24
  30.4 71.8 %collective-permute-start.5 = (f32[240,256]{1,0:T(8,128)}, f32[240,256]{1,0:T(8,128)}, u32[]{:S(2)}, u32[]{:S(2)}) collective-permute-start(f32[240,256]{1,0:T(8,128)} %collective-permute-done.3), channel_id=1, source_target_pairs={{64,256},{320,0},{65,257},{321,1},{66,258},{322,2},{67,259},{323,3... | collective-permute-start | bytes 737288 | tf_op jit(solution)/shard_map/ppermute | solution.py:24
  31.7 70.5 %collective-permute-start.6 = (f32[240,256]{1,0:T(8,128)}, f32[240,256]{1,0:T(8,128)}, u32[]{:S(2)}, u32[]{:S(2)}) collective-permute-start(f32[240,256]{1,0:T(8,128)} %collective-permute-done.1), channel_id=1, source_target_pairs={{0,256},{256,0},{1,257},{257,1},{2,258},{258,2},{3,259},{259,3},{4... | collective-permute-start | bytes 737288 | tf_op jit(solution)/shard_map/ppermute | solution.py:24
  46.4 0.7 copy-start.5
  81.3 10.3 %all-to-all-start.1 = ((f32[8,32,256]{2,1,0:T(8,128)}), f32[8,32,256]{2,1,0:T(8,128)S(1)}, u32[]{:S(2)}, u32[]{:S(2)}) async-start(f32[8,32,256]{2,1,0:T(8,128)} %broadcast_in_dim.7), calls=%async_computation.1 | async-start | bytes 524288 | tf_op jit(solution)/shard_map/cond/branch_1_fun/all_to_all | solution.py:52
  102.1 0.6 copy-start.1
  102.1 0.6 copy-start.3
  116.7 7.4 %copy-start.4 = (f32[48,128]{1,0:T(8,128)S(1)}, f32[48,128]{1,0:T(8,128)}, u32[]{:S(2)}) copy-start(f32[48,128]{1,0:T(8,128)} %copy-done.3) | copy-start | bytes 73732
  116.7 17.7 %all-to-all-start.4 = ((f32[8,32,128]{2,1,0:T(8,128)}), f32[8,32,128]{2,1,0:T(8,128)S(1)}, u32[]{:S(2)}, u32[]{:S(2)}) async-start(f32[8,32,128]{2,1,0:T(8,128)} %broadcast_in_dim.15), calls=%async_computation.4 | async-start | bytes 262144 | tf_op jit(solution)/shard_map/all_to_all | solution.py:52
  124.1 15.4 %collective-permute-start.8 = (f32[48,128]{1,0:T(8,128)S(1)}, f32[48,128]{1,0:T(8,128)S(1)}, u32[]{:S(2)}, u32[]{:S(2)}) collective-permute-start(f32[48,128]{1,0:T(8,128)S(1)} %copy-done.4), channel_id=1, source_target_pairs={{0,64},{64,128},{128,192},{192,256},{256,320},{320,384},{384,448},... | collective-permute-start | bytes 73736 | tf_op jit(solution)/shard_map/ppermute | solution.py:24
  140.2 13.2 %all-to-all-start.5 = ((f32[8,80,128]{2,1,0:T(8,128)}), f32[8,80,128]{2,1,0:T(8,128)S(1)}, u32[]{:S(2)}, u32[]{:S(2)}) async-start(f32[8,80,128]{2,1,0:T(8,128)} %broadcast_in_dim.16), calls=%async_computation.5 | async-start | bytes 655360 | tf_op jit(solution)/shard_map/all_to_all | solution.py:52
  153.9 0.8 copy-start.2

commit v3 on v1

v3 whole, which is shorter than its diff:
```python
import functools

import jax
import jax.numpy as jnp
from jax import lax
from jax.experimental import pallas as pl
from jax.experimental.pallas import tpu as pltpu
from jax.sharding import Mesh, PartitionSpec as P

SWEEPS = 4


STEP_GAIN = 3.0
EPSILON = 1e-06

NEAR = ("y", "core")
FAR = "z_lo"
ROW = ("z_lo", "y", "core")
COL = ("z_hi", "x")


DIRECT, RING, TWO, ONE = 304, 240, 240, 240


def send(shard, pairs):
    return lax.ppermute(shard, COL, pairs)


def inside(source, target):
    return [(source, target), (4 + source, 4 + target)]


def across(source, target):
    return [(source, 4 + target), (4 + source, target)]


def product(left, right):
    return jnp.dot(left, right, precision=lax.Precision.HIGH, preferred_element_type=jnp.float32)


def inner_gram(left, right):
    return lax.dot_general(
        left,
        right,
        (((0,), (0,)), ((), ())),
        precision=lax.Precision.HIGH,
        preferred_element_type=jnp.float32,
    )


def spread(piece, axis):
    peers = lax.axis_size(axis)
    copies = jnp.broadcast_to(piece[None], (peers,) + piece.shape)
    return lax.all_to_all(copies, axis, 0, 0, tiled=True)


def near_sum(part):
    near = lax.axis_size(NEAR)
    slices = part.reshape(near, part.shape[0] // near, part.shape[1])
    return jnp.sum(lax.all_to_all(slices, NEAR, 0, 0, tiled=True), axis=0)


def far_sum(piece):
    return jnp.sum(spread(piece, FAR), axis=0)


ALONG = (((1,), (0,)), ((), ()))
DOWN = (((0,), (0,)), ((), ()))


def halves(value):
    high = value.astype(jnp.bfloat16)
    return high, (value - high.astype(jnp.float32)).astype(jnp.bfloat16)


def times(left, right, dims=ALONG):
    def dot(one, other):
        return lax.dot_general(one, other, dims, preferred_element_type=jnp.float32)

    return dot(left[0], right[0]) + (dot(left[0], right[1]) + dot(left[1], right[0]))


def picks(left, chosen, dims=ALONG):
    def dot(one):
        return lax.dot_general(one, chosen, dims, preferred_element_type=jnp.float32)

    return dot(left[0]) + dot(left[1])


def diagonal(value):
    width = value.shape[0]
    down = lax.broadcasted_iota(jnp.int32, (width, width), 0)
    along = lax.broadcasted_iota(jnp.int32, (width, width), 1)
    return jnp.where(down == along, value, 0.0)


def swept(gram, last_gram):
    width = gram.shape[0]
    scale = jnp.sum(jnp.sum(diagonal(gram), axis=0, keepdims=True), axis=1, keepdims=True) / width
    scaled = gram / scale
    down = lax.broadcasted_iota(jnp.int32, (width, width), 0)
    along = lax.broadcasted_iota(jnp.int32, (width, width), 1)
    steps = (along - down).astype(jnp.float32) * (STEP_GAIN / width / width)
    ident = jnp.where(down == along, 1.0, 0.0)
    basis = ident
    for sweep in range(SWEEPS):
        skew = scaled * steps
        pair = halves(skew)
        square = 0.5 * times(pair, pair)
        move = skew + square
        moves = halves(move)
        half_way = scaled + times(halves(scaled), moves)
        basis = ident + move if sweep == 0 else basis + times(halves(basis), moves)
        if sweep < SWEEPS - 1 or last_gram:
            scaled = half_way + times(halves(square - skew), halves(half_way))
    if last_gram:
        return basis, scaled * scale
    return basis, jnp.sum((ident + move) * half_way, axis=0, keepdims=True) * scale


def whole_gram(upper, between, lower):
    return jnp.concatenate(
        [
            jnp.concatenate([upper, between], axis=1),
            jnp.concatenate([between.T, lower], axis=1),
        ],
        axis=0,
    )


def picked(blocks, order, first):
    half = blocks.shape[1]
    gram = whole_gram(blocks[:half], blocks[half : 2 * half], blocks[2 * half :])
    basis, moved = swept(gram, True)
    down = lax.broadcasted_iota(jnp.int32, (2 * half, half), 0)
    chosen = jnp.where(down == order[:, first : first + half], 1.0, 0.0).astype(jnp.bfloat16)
    columns = halves(picks(halves(moved), chosen))
    return picks(halves(basis), chosen), picks(columns, chosen, DOWN)


def first_kernel(blocks_ref, order_ref, kept_ref, gram_ref):
    half = blocks_ref.shape[2]
    kept_ref[...], gram_ref[...] = picked(blocks_ref[...].reshape(3 * half, half), order_ref[...], 0)


def sweep_first(blocks, order):
    half = blocks.shape[2]
    return pl.pallas_call(
        first_kernel,
        out_shape=(
            jax.ShapeDtypeStruct((2 * half, half), jnp.float32),
            jax.ShapeDtypeStruct((half, half), jnp.float32),
        ),
        compiler_params=pltpu.CompilerParams(vmem_limit_bytes=40 * 2**20),
        name="sweep_first",
    )(blocks, order)


def last_kernel(rows, sums_ref, order_ref, kept_ref, gram_ref, own_ref, behind_ref,
                out_ref, norm_ref, own_high, own_low, behind_high, behind_low):
    half = kept_ref.shape[1]
    share = 2 * half // sums_ref.shape[0]

    @pl.when(pl.program_id(0) == 0)
    def _():
        given, given_gram = picked(sums_ref[:, share:, :].reshape(3 * half, half), order_ref[...], half)
        given = halves(given)
        cross = halves(sums_ref[:, :share, :].reshape(2 * half, half))
        between = times(cross, given, DOWN)
        basis, squares = swept(whole_gram(gram_ref[...], between, given_gram), False)
        norm_ref[...] = jnp.sqrt(jnp.maximum(squares, 0.0) / rows + EPSILON)
        own_high[...], own_low[...] = halves(times(halves(kept_ref[...]), halves(basis[:half])))
        behind_high[...], behind_low[...] = halves(times(given, halves(basis[half:])))

    out_ref[...] = times(halves(own_ref[...]), (own_high[...], own_low[...])) + times(
        halves(behind_ref[...]), (behind_high[...], behind_low[...])
    )


def sweep_last(rows, sums, order, kept, gram, own, behind):
    width = own.shape[1]
    tile = 256
    full = lambda value: pl.BlockSpec(value.shape, lambda step: (0,) * value.ndim)
    tiles = pl.BlockSpec((tile, width), lambda step: (step, 0))
    small = (sums, order, kept, gram)
    return pl.pallas_call(
        functools.partial(last_kernel, rows),
        grid=(own.shape[0] // tile,),
        in_specs=[full(value) for value in small] + [tiles, tiles],
        out_specs=(tiles, pl.BlockSpec((1, width), lambda step: (0, 0))),
        out_shape=(jax.ShapeDtypeStruct(own.shape, jnp.float32), jax.ShapeDtypeStruct((1, width), jnp.float32)),
        scratch_shapes=[pltpu.VMEM((width, width), jnp.bfloat16)] * 4,
        compiler_params=pltpu.CompilerParams(vmem_limit_bytes=40 * 2**20),
        name="sweep_last",
    )(*small, own, behind)


def first_blocks(matrix):
    half = matrix.shape[1] // 2
    top = inner_gram(matrix[:, :half], matrix)
    return jnp.concatenate(
        [top[:, :half], top[:, half:], inner_gram(matrix[:, half:], matrix[:, half:])], axis=0
    )


def shards(matrix, keep):
    rows, width = matrix.shape
    half = width // 2
    place = lax.axis_index("x")
    part, whole = lax.optimization_barrier((first_blocks(matrix), matrix))
    direct, _, two, one = jnp.split(whole, [DIRECT, DIRECT + RING, DIRECT + RING + TWO])
    turned = send(whole[DIRECT:], sum([inside(i, (i + 1) % 4) for i in range(4)], []))
    at_two = send(two, inside(3, 2))
    at_one = send(one, inside(3, 1))
    slices = near_sum(part)
    turned, at_two, at_one, slices = lax.optimization_barrier((turned, at_two, at_one, slices))
    crossed_two = send(at_two, across(2, 0))
    crossed_one = send(at_one, across(1, 0))
    crossed_ring = send(turned[:RING], across(0, 0))
    direct = send(direct, [(i, (i + 1) % 8) for i in range(8)])
    slices = far_sum(slices)
    share = slices.shape[0]
    order = jnp.broadcast_to(keep.astype(jnp.float32).reshape(2, half)[None], (4, 2, half)).reshape(8, half)
    arrived = send(jnp.concatenate([slices, order], axis=0), [(i, (i + 1) % 8) for i in range(8)])

    def turn_first(slices, keep):
        return sweep_first(spread(slices, NEAR), keep)

    kept_basis, kept_gram = lax.cond(
        keep[0, 0] >= 0,
        turn_first,
        lambda *_: (jnp.zeros((width, half), jnp.float32), jnp.zeros((half, half), jnp.float32)),
        slices,
        keep,
    )

    direct, crossed_ring, crossed_two, crossed_one, arrived, kept_basis = lax.optimization_barrier(
        (direct, crossed_ring, crossed_two, crossed_one, arrived, kept_basis)
    )
    crossed = jnp.concatenate([crossed_ring, crossed_two, crossed_one], axis=0)
    behind = jnp.concatenate([direct, jnp.where(place == 0, crossed, turned)], axis=0)
    cross = far_sum(product(near_sum(inner_gram(behind, matrix)), kept_basis))
    sums = spread(jnp.concatenate([cross, arrived[:share]], axis=0), NEAR)
    behind_keep = arrived[share : share + 2].reshape(1, width).astype(jnp.int32)
    total_rows = rows * lax.axis_size(ROW)
    rotated, norms = sweep_last(total_rows, sums, behind_keep, kept_basis, kept_gram, matrix, behind)
    return (rotated, norms.reshape(width))


def solution(mesh):
    fine = Mesh(mesh.devices.reshape(2, 4, 8, 4, 2), ("z_hi", "x", "z_lo", "y", "core"))
    return jax.shard_map(
        shards,
        mesh=fine,
        in_specs=(P(ROW, COL), P(COL, None)),
        out_specs=(P(ROW, COL), P(COL)),
        check_vma=False,
    )
```

time: 176 us -> 149 us (0.85)
  waiting for transfers between devices: 71.3 us -> 16.7 us
  starting transfers between devices: 33.8 us -> 65 us
  matrix products: 23.4 us -> 5.06 us
  Pallas kernels: 0 us -> 16.6 us
  local copies, waits for them, and re-layouts: 6.38 us -> 4.13 us
    ppermute x2 -> x8, waiting for transfers between devices: 48 us -> 0.02 us  [send(): return lax.ppermute(shard, COL, pairs)]
    ppermute x2 -> x8, starting transfers between devices: 5.22 us -> 27.1 us  [send(): return lax.ppermute(shard, COL, pairs)]
    pallas_call x0 -> x2, Pallas kernels: none -> 16.6 us  [the longest x1 12.1 us: sweep_last(): pl.pallas_call(functools.partial(last_kernel, rows), grid=(own.shape[0] /...]
    dot_general x29 -> x1, matrix products: 15.1 us -> 0.16 us  [product(): jnp.dot(left, right, precision=lax.Precision.HIGH, preferred_element_type...]
    all_to_all x3, starting transfers between devices: 23.9 us -> 37.9 us  [spread(): return lax.all_to_all(copies, axis, 0, 0, tiled=True)]
    all_to_all x1 -> x2, blocking collectives: 15.8 us -> 24.5 us  [near_sum(): return jnp.sum(lax.all_to_all(slices, NEAR, 0, 0, tiled=True), axis=0)]
    all_to_all x1, blocking collectives: 20.4 us -> 13.4 us  [spread(): return lax.all_to_all(copies, axis, 0, 0, tiled=True)]
    all_to_all x1 -> x0, starting transfers between devices: 4.68 us -> none  [row_sum(): mine = jnp.sum(lax.all_to_all(slices, NEAR, 0, 0, tiled=True), axis=0)]
  transfers between devices with their start and end apart: 6 -> 11, of which waited for: 5 -> 2; matrix products, arithmetic and copies ran while one was open for 1% -> 0% of each run, Pallas kernels for 0% -> 3%
where the time goes in v3:
time: 149 us
  starting transfers between devices  65 us (44%)
  blocking collectives  37.9 us (25%)
  waiting for transfers between devices  16.7 us (11%)
  Pallas kernels  16.6 us (11%)
  matrix products  5.06 us (3%)
  local copies, waits for them, and re-layouts  4.13 us (3%)
  between operations  1.64 us (1%)
    all_to_all x3, starting transfers between devices, spread(): return lax.all_to_all(copies, axis, 0, 0, tiled=True)  37.9 us
    ppermute x8, starting transfers between devices, send(): return lax.ppermute(shard, COL, pairs)  27.1 us
    all_to_all x2, blocking collectives, near_sum(): return jnp.sum(lax.all_to_all(slices, NEAR, 0, 0, tiled=True), axis=0)  24.5 us
    all_to_all x3, waiting for transfers between devices, spread(): return lax.all_to_all(copies, axis, 0, 0, tiled=True)  16.7 us
    all_to_all x1, blocking collectives, spread(): return lax.all_to_all(copies, axis, 0, 0, tiled=True)  13.4 us
    pallas_call x1, Pallas kernels, sweep_last(): pl.pallas_call(functools.partial(last_kernel, rows), grid=(own.shape[0] /...  12.1 us
    dot_general x3, matrix products, inner_gram(): lax.dot_general(left, right, (((0,), (0,)), ((), ())), precision=lax.Prec...  4.9 us
    pallas_call x1, Pallas kernels, sweep_first(): pl.pallas_call(first_kernel, out_shape=(jax.ShapeDtypeStruct((2 * half, h...  4.54 us
  transfers between devices with their start and end apart: 11, of which 2 were waited for; matrix products, arithmetic and copies ran while one was open for 0% of the time, Pallas kernels for 3%

profile of v3, /device:TPU:1, one launch (start us, length us, event | category | flops | bytes accessed | tf_op | source)
XLA Modules:
  0.0 148.6 jit_solution(11029960057133772117)
XLA Ops:
  0.6 1.9 %fusion = f32[128,128]{1,0:T(8,128)S(1)} fusion(f32[1024,256]{1,0:T(8,128)} %own_ref.1), kind=kOutput, calls=%fused_computation.2 | convolution fusion | flops 100663296 | bytes 589824 | tf_op jit(solution)/shard_map/dot_general | solution.py:42
  2.5 0.0 copy-start
  2.5 2.1 %fusion.2 = f32[128,256]{1,0:T(8,128)S(1)} fusion(f32[1024,256]{1,0:T(8,128)} %own_ref.1), kind=kOutput, calls=%fused_computation.4 | convolution fusion | flops 201326592 | bytes 1703936 | tf_op jit(solution)/shard_map/dot_general | solution.py:42
  4.6 0.0 copy-done
  4.7 3.9 %collective-permute-start.1 = (f32[720,256]{1,0:T(8,128)S(1)}, f32[720,256]{1,0:T(8,128)S(1)}, u32[]{:S(2)}, u32[]{:S(2)}) collective-permute-start(f32[720,256]{1,0:T(8,128)S(1)} %slice.32), channel_id=1, source_target_pairs={{0,64},{256,320},{64,128},{320,384},{128,192},{384,448},{192,0},{4... | collective-permute-start | bytes 2211848 | tf_op jit(solution)/shard_map/ppermute | solution.py:26
  8.7 0.7 collective-permute-start.3
  9.4 1.4 collective-permute-start.2
  10.7 13.1 %all_to_all.30 = f32[8,48,128]{2,1,0:T(8,128)S(1)} all-to-all(f32[8,48,128]{2,1,0:T(8,128)S(1)} %bitcast.13), channel_id=1, replica_groups=mesh['z_hi'=2,'x'=4,'z_lo'=8,'y'=4,'core'=2] {'y','core'}, dimensions={0} | all-to-all | bytes 393216 | tf_op jit(solution)/shard_map/all_to_all | solution.py:60
  23.9 0.0 collective-permute-done.3
  23.9 0.0 copy-start.5
  23.9 0.0 collective-permute-done.2
  23.9 0.0 collective-permute-done.1
  23.9 0.7 broadcast_in_dim.16
  24.6 0.0 copy-done.5
  24.6 14.3 %all-to-all-start.2 = ((f32[8,48,128]{2,1,0:T(8,128)}), f32[8,48,128]{2,1,0:T(8,128)S(1)}, u32[]{:S(2)}, u32[]{:S(2)}) async-start(f32[8,48,128]{2,1,0:T(8,128)} %broadcast_in_dim.16), calls=%async_computation.2 | async-start | bytes 393216 | tf_op jit(solution)/shard_map/all_to_all | solution.py:54
  38.9 0.0 copy-start.6
  38.9 0.0 copy-start.4
  39.0 2.1 %collective-permute-start = (f32[304,256]{1,0:T(8,128)S(1)}, f32[304,256]{1,0:T(8,128)S(1)}, u32[]{:S(2)}, u32[]{:S(2)}) collective-permute-start(f32[304,256]{1,0:T(8,128)S(1)} %split.9), channel_id=1, source_target_pairs={{0,64},{64,128},{128,192},{192,256},{256,320},{320,384},{384,448},... | collective-permute-start | bytes 933896 | tf_op jit(solution)/shard_map/ppermute | solution.py:26
  41.0 7.9 %collective-permute-start.4 = (f32[240,256]{1,0:T(8,128)S(1)}, f32[240,256]{1,0:T(8,128)}, u32[]{:S(2)}, u32[]{:S(2)}) collective-permute-start(f32[240,256]{1,0:T(8,128)S(1)} %slice.33), channel_id=1, source_target_pairs={{0,256},{256,0},{1,257},{257,1},{2,258},{258,2},{3,259},{259,3},{4... | collective-permute-start | bytes 737288 | tf_op jit(solution)/shard_map/ppermute | solution.py:26
  49.0 1.3 collective-permute-start.5
  50.3 0.0 copy-done.6
  50.3 1.3 collective-permute-start.6
  51.6 0.0 copy-done.4
  51.6 0.0 all-to-all-done.2
  51.7 8.5 %collective-permute-start.7 = (f32[56,128]{1,0:T(8,128)S(1)}, f32[56,128]{1,0:T(8,128)S(1)}, u32[]{:S(2)}, u32[]{:S(2)}) collective-permute-start(f32[56,128]{1,0:T(8,128)S(1)} %pad_maximum_fusion.3), channel_id=1, source_target_pairs={{0,64},{64,128},{128,192},{192,256},{256,320},{320,384},{384,448},... | collective-permute-start | bytes 86024 | tf_op jit(solution)/shard_map/ppermute | solution.py:26
  60.2 0.5 slice.34
  61.4 18.0 %conditional.1 = ((f32[256,128]{1,0:T(8,128)S(1)}, f32[128,128]{1,0:T(8,128)S(1)})) conditional(s32[]{:T(128)} %bitcast.3, () %tuple.20, (f32[48,128]{1,0:T(8,128)S(1)}, s32[1,256]{1,0:T(1,128)S(1)}) %tuple.30), branch_computations={%region_2.0_spmd, %region_3.0_spmd} | conditional | bytes 614408 | solution.py:229
  61.4 13.4 %all_to_all.29.blocks_ref = f32[8,48,128]{2,1,0:T(8,128)S(1)} all-to-all(f32[8,48,128]{2,1,0:T(8,128)S(1)} %broadcast_in_dim.1), channel_id=1, replica_groups=mesh['z_hi'=2,'x'=4,'z_lo'=8,'y'=4,'core'=2] {'y','core'}, dimensions={0} | all-to-all | bytes 393216 | tf_op jit(solution)/shard_map/cond/branch_1_fun/all_to_all | solution.py:54
  74.8 4.5 %sweep_first.1 = (f32[256,128]{1,0:T(8,128)S(1)}, f32[128,128]{1,0:T(8,128)S(1)}) custom-call(f32[8,48,128]{2,1,0:T(8,128)S(1)} %all_to_all.29.blocks_ref, s32[1,256]{1,0:T(1,128)S(1)} %get-tuple-element.5.order_ref), custom_call_target="tpu_custom_call" | custom-call | tf_op jit(solution)/shard_map/cond/branch_1_fun/sweep_first/pallas_call | solution.py:148
  79.3 0.0 copy-start.1
  79.4 0.0 collective-permute-done
  79.4 0.0 collective-permute-done.4
  79.4 0.0 collective-permute-done.5
  79.4 0.0 collective-permute-done.6
  79.4 0.0 collective-permute-done.7
  79.4 0.0 copy-start.2
  79.4 0.6 copy-done.2
  80.0 1.3 maximum_select_fusion
  81.3 1.0 fusion.4
  82.3 11.4 %all_to_all.31 = f32[8,32,256]{2,1,0:T(8,128)S(1)} all-to-all(f32[8,32,256]{2,1,0:T(8,128)S(1)} %bitcast.12), channel_id=1, replica_groups=mesh['z_hi'=2,'x'=4,'z_lo'=8,'y'=4,'core'=2] {'y','core'}, dimensions={0} | all-to-all | bytes 524288 | tf_op jit(solution)/shard_map/all_to_all | solution.py:60
  93.7 0.0 copy-done.1
  93.8 0.2 fusion.7
  93.9 0.7 broadcast_in_dim.19
  94.6 17.8 %all-to-all-start.4 = ((f32[8,32,128]{2,1,0:T(8,128)}), f32[8,32,128]{2,1,0:T(8,128)S(1)}, u32[]{:S(2)}, u32[]{:S(2)}) async-start(f32[8,32,128]{2,1,0:T(8,128)} %broadcast_in_dim.19), calls=%async_computation.4 | async-start | bytes 262144 | tf_op jit(solution)/shard_map/all_to_all | solution.py:54
  112.4 0.0 slice-start
  112.4 10.3 %all-to-all-done.4 = f32[8,32,128]{2,1,0:T(8,128)S(1)} async-done(((f32[8,32,128]{2,1,0:T(8,128)}), f32[8,32,128]{2,1,0:T(8,128)S(1)}, u32[]{:S(2)}, u32[]{:S(2)}) %all-to-all-start.4) | async-done | bytes 131104 | tf_op jit(solution)/shard_map/all_to_all | solution.py:54
  122.7 0.0 slice-done
  122.7 0.7 broadcast_in_dim.20
  123.5 5.9 %all-to-all-start.5 = ((f32[8,80,128]{2,1,0:T(8,128)}), f32[8,80,128]{2,1,0:T(8,128)S(1)}, u32[]{:S(2)}, u32[]{:S(2)}) async-start(f32[8,80,128]{2,1,0:T(8,128)} %broadcast_in_dim.20), calls=%async_computation.5 | async-start | bytes 655360 | tf_op jit(solution)/shard_map/all_to_all | solution.py:54
  129.3 0.0 copy-start.3
  129.3 0.1 pad_maximum_fusion.behind_ref
  129.4 0.7 copy-done.3
  130.1 6.4 %all-to-all-done.5.sums_ref = f32[8,80,128]{2,1,0:T(8,128)S(1)} async-done(((f32[8,80,128]{2,1,0:T(8,128)}), f32[8,80,128]{2,1,0:T(8,128)S(1)}, u32[]{:S(2)}, u32[]{:S(2)}) %all-to-all-start.5) | async-done | bytes 327712 | tf_op jit(solution)/shard_map/all_to_all | solution.py:54
  136.5 12.1 %sweep_last.1 = (f32[1024,256]{1,0:T(8,128)}, f32[1,256]{1,0:T(1,128)}) custom-call(f32[8,80,128]{2,1,0:T(8,128)S(1)} %all-to-all-done.5.sums_ref, s32[1,256]{1,0:T(1,128)S(1)} %bitcast.11, f32[256,128]{1,0:T(8,128)} %copy-done.1, f32[128,128]{1,0:T(8,128)S(1)} %get-tuple-element.37.gram_ref, f32[1024,256]{1,0:T(8,128)S(1)} %copy-done, ...), custom_call_target="tpu_custom_call" | custom-call | tf_op jit(solution)/shard_map/sweep_last/pallas_call | solution.py:186
  (16 shorter events, 0.3 us)
Async XLA Ops:
  2.5 2.1 %copy-start = (f32[1024,256]{1,0:T(8,128)S(1)}, f32[1024,256]{1,0:T(8,128)}, u32[]{:S(2)}) copy-start(f32[1024,256]{1,0:T(8,128)} %own_ref.1) | copy-start | bytes 3145732
  4.7 19.2 %collective-permute-start.1 = (f32[720,256]{1,0:T(8,128)S(1)}, f32[720,256]{1,0:T(8,128)S(1)}, u32[]{:S(2)}, u32[]{:S(2)}) collective-permute-start(f32[720,256]{1,0:T(8,128)S(1)} %slice.32), channel_id=1, source_target_pairs={{0,64},{256,320},{64,128},{320,384},{128,192},{384,448},{192,0},{4... | collective-permute-start | bytes 2211848 | tf_op jit(solution)/shard_map/ppermute | solution.py:26
  8.7 15.2 %collective-permute-start.3 = (f32[240,256]{1,0:T(8,128)S(1)}, f32[240,256]{1,0:T(8,128)S(1)}, u32[]{:S(2)}, u32[]{:S(2)}) collective-permute-start(f32[240,256]{1,0:T(8,128)S(1)} %get-tuple-element.40), channel_id=1, source_target_pairs={{192,64},{448,320},{193,65},{449,321},{194,66},{450,322},{195,67},... | collective-permute-start | bytes 737288 | tf_op jit(solution)/shard_map/ppermute | solution.py:26
  9.4 14.5 %collective-permute-start.2 = (f32[240,256]{1,0:T(8,128)S(1)}, f32[240,256]{1,0:T(8,128)}, u32[]{:S(2)}, u32[]{:S(2)}) collective-permute-start(f32[240,256]{1,0:T(8,128)S(1)} %get-tuple-element.41), channel_id=1, source_target_pairs={{192,128},{448,384},{193,129},{449,385},{194,130},{450,386},{195,1... | collective-permute-start | bytes 737288 | tf_op jit(solution)/shard_map/ppermute | solution.py:26
  23.9 0.8 copy-start.5
  24.6 27.0 %all-to-all-start.2 = ((f32[8,48,128]{2,1,0:T(8,128)}), f32[8,48,128]{2,1,0:T(8,128)S(1)}, u32[]{:S(2)}, u32[]{:S(2)}) async-start(f32[8,48,128]{2,1,0:T(8,128)} %broadcast_in_dim.16), calls=%async_computation.2 | async-start | bytes 393216 | tf_op jit(solution)/shard_map/all_to_all | solution.py:54
  38.9 11.4 %copy-start.6 = (f32[240,256]{1,0:T(8,128)S(1)}, f32[240,256]{1,0:T(8,128)}, u32[]{:S(2)}) copy-start(f32[240,256]{1,0:T(8,128)} %copy-done.5) | copy-start | bytes 737284
  38.9 12.7 %copy-start.4 = (s32[1,256]{1,0:T(1,128)S(1)}, s32[1,256]{1,0:T(1,128)}, u32[]{:S(2)}) copy-start(s32[1,256]{1,0:T(1,128)} %param.5) | copy-start | bytes 3076
  39.0 40.4 %collective-permute-start = (f32[304,256]{1,0:T(8,128)S(1)}, f32[304,256]{1,0:T(8,128)S(1)}, u32[]{:S(2)}, u32[]{:S(2)}) collective-permute-start(f32[304,256]{1,0:T(8,128)S(1)} %split.9), channel_id=1, source_target_pairs={{0,64},{64,128},{128,192},{192,256},{256,320},{320,384},{384,448},... | collective-permute-start | bytes 933896 | tf_op jit(solution)/shard_map/ppermute | solution.py:26
  41.0 38.3 %collective-permute-start.4 = (f32[240,256]{1,0:T(8,128)S(1)}, f32[240,256]{1,0:T(8,128)}, u32[]{:S(2)}, u32[]{:S(2)}) collective-permute-start(f32[240,256]{1,0:T(8,128)S(1)} %slice.33), channel_id=1, source_target_pairs={{0,256},{256,0},{1,257},{257,1},{2,258},{258,2},{3,259},{259,3},{4... | collective-permute-start | bytes 737288 | tf_op jit(solution)/shard_map/ppermute | solution.py:26
  49.0 30.4 %collective-permute-start.5 = (f32[240,256]{1,0:T(8,128)}, f32[240,256]{1,0:T(8,128)}, u32[]{:S(2)}, u32[]{:S(2)}) collective-permute-start(f32[240,256]{1,0:T(8,128)} %collective-permute-done.2), channel_id=1, source_target_pairs={{128,256},{384,0},{129,257},{385,1},{130,258},{386,2},{131,259},{3... | collective-permute-start | bytes 737288 | tf_op jit(solution)/shard_map/ppermute | solution.py:26
  50.3 29.1 %collective-permute-start.6 = (f32[240,256]{1,0:T(8,128)S(1)}, f32[240,256]{1,0:T(8,128)}, u32[]{:S(2)}, u32[]{:S(2)}) collective-permute-start(f32[240,256]{1,0:T(8,128)S(1)} %copy-done.6), channel_id=1, source_target_pairs={{64,256},{320,0},{65,257},{321,1},{66,258},{322,2},{67,259},{323,3... | collective-permute-start | bytes 737288 | tf_op jit(solution)/shard_map/ppermute | solution.py:26
  51.7 27.7 %collective-permute-start.7 = (f32[56,128]{1,0:T(8,128)S(1)}, f32[56,128]{1,0:T(8,128)S(1)}, u32[]{:S(2)}, u32[]{:S(2)}) collective-permute-start(f32[56,128]{1,0:T(8,128)S(1)} %pad_maximum_fusion.3), channel_id=1, source_target_pairs={{0,64},{64,128},{128,192},{192,256},{256,320},{320,384},{384,448},... | collective-permute-start | bytes 86024 | tf_op jit(solution)/shard_map/ppermute | solution.py:26
  79.3 14.4 %copy-start.1 = (f32[256,128]{1,0:T(8,128)}, f32[256,128]{1,0:T(8,128)S(1)}, u32[]{:S(2)}) copy-start(f32[256,128]{1,0:T(8,128)S(1)} %get-tuple-element.35.kept_ref) | copy-start | bytes 393220
  79.4 0.6 copy-start.2
  94.6 28.1 %all-to-all-start.4 = ((f32[8,32,128]{2,1,0:T(8,128)}), f32[8,32,128]{2,1,0:T(8,128)S(1)}, u32[]{:S(2)}, u32[]{:S(2)}) async-start(f32[8,32,128]{2,1,0:T(8,128)} %broadcast_in_dim.19), calls=%async_computation.4 | async-start | bytes 262144 | tf_op jit(solution)/shard_map/all_to_all | solution.py:54
  112.4 10.3 %slice-start = ((f32[56,128]{1,0:T(8,128)}), f32[48,128]{1,0:T(8,128)S(1)}, s32[]{:S(2)}) async-start(f32[56,128]{1,0:T(8,128)} %copy-done.2), calls=%async_computation.6 | async-start | bytes 49152 | tf_op jit(solution)/shard_map/slice | solution.py:243
  123.5 13.0 %all-to-all-start.5 = ((f32[8,80,128]{2,1,0:T(8,128)}), f32[8,80,128]{2,1,0:T(8,128)S(1)}, u32[]{:S(2)}, u32[]{:S(2)}) async-start(f32[8,80,128]{2,1,0:T(8,128)} %broadcast_in_dim.20), calls=%async_computation.5 | async-start | bytes 655360 | tf_op jit(solution)/shard_map/all_to_all | solution.py:54
  129.3 0.7 copy-start.3

commit v4 on v3

--- a/solution.py
+++ b/solution.py
@@ -19,7 +19,7 @@
 COL = ("z_hi", "x")
 
 
-DIRECT, RING, TWO, ONE = 304, 240, 240, 240
+DIRECT, RING, TWO, ONE = 216, 256, 280, 272
 
 
 def send(shard, pairs):
@@ -138,36 +138,34 @@
     return picks(halves(basis), chosen), picks(columns, chosen, DOWN)
 
 
-def first_kernel(blocks_ref, order_ref, kept_ref, gram_ref):
+def turn_kernel(first, blocks_ref, order_ref, basis_ref, gram_ref):
     half = blocks_ref.shape[2]
-    kept_ref[...], gram_ref[...] = picked(blocks_ref[...].reshape(3 * half, half), order_ref[...], 0)
-
-
-def sweep_first(blocks, order):
+    basis_ref[...], gram_ref[...] = picked(blocks_ref[...].reshape(3 * half, half), order_ref[...], first)
+
+
+def turn_pair(blocks, order, first):
     half = blocks.shape[2]
     return pl.pallas_call(
-        first_kernel,
+        functools.partial(turn_kernel, first),
         out_shape=(
             jax.ShapeDtypeStruct((2 * half, half), jnp.float32),
             jax.ShapeDtypeStruct((half, half), jnp.float32),
         ),
         compiler_params=pltpu.CompilerParams(vmem_limit_bytes=40 * 2**20),
-        name="sweep_first",
+        cost_estimate=pl.CostEstimate(flops=5 * 10**9, bytes_accessed=4 * 10**5, transcendentals=0),
+        name="turn_pair",
     )(blocks, order)
 
 
-def last_kernel(rows, sums_ref, order_ref, kept_ref, gram_ref, own_ref, behind_ref,
+def last_kernel(rows, cross_ref, kept_ref, gram_ref, given_ref, given_gram_ref, own_ref, behind_ref,
                 out_ref, norm_ref, own_high, own_low, behind_high, behind_low):
     half = kept_ref.shape[1]
-    share = 2 * half // sums_ref.shape[0]
 
     @pl.when(pl.program_id(0) == 0)
     def _():
-        given, given_gram = picked(sums_ref[:, share:, :].reshape(3 * half, half), order_ref[...], half)
-        given = halves(given)
-        cross = halves(sums_ref[:, :share, :].reshape(2 * half, half))
-        between = times(cross, given, DOWN)
-        basis, squares = swept(whole_gram(gram_ref[...], between, given_gram), False)
+        given = halves(given_ref[...])
+        between = times(halves(cross_ref[...].reshape(2 * half, half)), given, DOWN)
+        basis, squares = swept(whole_gram(gram_ref[...], between, given_gram_ref[...]), False)
         norm_ref[...] = jnp.sqrt(jnp.maximum(squares, 0.0) / rows + EPSILON)
         own_high[...], own_low[...] = halves(times(halves(kept_ref[...]), halves(basis[:half])))
         behind_high[...], behind_low[...] = halves(times(given, halves(basis[half:])))
@@ -177,12 +175,12 @@
     )
 
 
-def sweep_last(rows, sums, order, kept, gram, own, behind):
+def sweep_last(rows, cross, kept, gram, given, given_gram, own, behind):
     width = own.shape[1]
     tile = 256
     full = lambda value: pl.BlockSpec(value.shape, lambda step: (0,) * value.ndim)
     tiles = pl.BlockSpec((tile, width), lambda step: (step, 0))
-    small = (sums, order, kept, gram)
+    small = (cross, kept, gram, given, given_gram)
     return pl.pallas_call(
         functools.partial(last_kernel, rows),
         grid=(own.shape[0] // tile,),
@@ -197,26 +195,24 @@
 
 def first_blocks(matrix):
     half = matrix.shape[1] // 2
-    top = inner_gram(matrix[:, :half], matrix)
-    return jnp.concatenate(
-        [top[:, :half], top[:, half:], inner_gram(matrix[:, half:], matrix[:, half:])], axis=0
-    )
+    gram = inner_gram(matrix, matrix)
+    return jnp.concatenate([gram[:half, :half], gram[:half, half:], gram[half:, half:]], axis=0)
 
 
 def shards(matrix, keep):
     rows, width = matrix.shape
     half = width // 2
     place = lax.axis_index("x")
-    part, whole = lax.optimization_barrier((first_blocks(matrix), matrix))
+    part, whole = first_blocks(matrix), matrix
     direct, _, two, one = jnp.split(whole, [DIRECT, DIRECT + RING, DIRECT + RING + TWO])
     turned = send(whole[DIRECT:], sum([inside(i, (i + 1) % 4) for i in range(4)], []))
     at_two = send(two, inside(3, 2))
     at_one = send(one, inside(3, 1))
     slices = near_sum(part)
-    turned, at_two, at_one, slices = lax.optimization_barrier((turned, at_two, at_one, slices))
+    at_two, at_one, slices = lax.optimization_barrier((at_two, at_one, slices))
+    crossed_ring = send(turned[:RING], across(0, 0))
     crossed_two = send(at_two, across(2, 0))
     crossed_one = send(at_one, across(1, 0))
-    crossed_ring = send(turned[:RING], across(0, 0))
     direct = send(direct, [(i, (i + 1) % 8) for i in range(8)])
     slices = far_sum(slices)
     share = slices.shape[0]
@@ -224,7 +220,7 @@
     arrived = send(jnp.concatenate([slices, order], axis=0), [(i, (i + 1) % 8) for i in range(8)])
 
     def turn_first(slices, keep):
-        return sweep_first(spread(slices, NEAR), keep)
+        return turn_pair(spread(slices, NEAR), keep, 0)
 
     kept_basis, kept_gram = lax.cond(
         keep[0, 0] >= 0,
@@ -239,11 +235,26 @@
     )
     crossed = jnp.concatenate([crossed_ring, crossed_two, crossed_one], axis=0)
     behind = jnp.concatenate([direct, jnp.where(place == 0, crossed, turned)], axis=0)
-    cross = far_sum(product(near_sum(inner_gram(behind, matrix)), kept_basis))
-    sums = spread(jnp.concatenate([cross, arrived[:share]], axis=0), NEAR)
+    near = lax.axis_size(NEAR)
+    cross = inner_gram(behind, matrix)
+    cut = width // near
+    parts = [cross[:, :half].reshape(near, cut, half), cross[:, half:].reshape(near, cut, half)]
+    parts.append(jnp.broadcast_to(arrived[None, :share], (near, share, half)))
+    parts = lax.all_to_all(jnp.concatenate(parts, axis=1), NEAR, 0, 0, tiled=True)
+    cross = jnp.sum(parts[:, : 2 * cut], axis=0)
+    cross = product(cross[:cut], kept_basis[:half]) + product(cross[cut:], kept_basis[half:])
     behind_keep = arrived[share : share + 2].reshape(1, width).astype(jnp.int32)
-    total_rows = rows * lax.axis_size(ROW)
-    rotated, norms = sweep_last(total_rows, sums, behind_keep, kept_basis, kept_gram, matrix, behind)
+    given_basis, given_gram = turn_pair(parts[:, 2 * cut :], behind_keep, half)
+    rotated, norms = sweep_last(
+        rows * lax.axis_size(ROW),
+        spread(far_sum(cross), NEAR),
+        kept_basis,
+        kept_gram,
+        given_basis,
+        given_gram,
+        matrix,
+        behind,
+    )
     return (rotated, norms.reshape(width))
 
 

time: 149 us -> 140 us (0.940)
  the two profiles are of different devices: /device:TPU:1 before, /device:TPU:2 now
where the time goes in v4:
time: 140 us; the launch traced here: 139 us
  starting transfers between devices  66.7 us (48%)
  blocking collectives  32.4 us (23%)
  Pallas kernels  16.5 us (12%)
  waiting for transfers between devices  11.9 us (8%)
  local copies, waits for them, and re-layouts  4.8 us (3%)
  other arithmetic  3.22 us (2%)
  matrix products  2.28 us (2%)
  between operations  1.59 us (1%)
    ppermute x8, starting transfers between devices, send(): return lax.ppermute(shard, COL, pairs)  41.7 us
    all_to_all x3, starting transfers between devices, spread(): return lax.all_to_all(copies, axis, 0, 0, tiled=True)  24.9 us
    all_to_all x1, blocking collectives, shards(): lax.all_to_all(jnp.concatenate(parts, axis=1), NEAR, 0, 0, tiled=True)  12.1 us
    all_to_all x3, waiting for transfers between devices, spread(): return lax.all_to_all(copies, axis, 0, 0, tiled=True)  11.9 us
    all_to_all x1, blocking collectives, near_sum(): return jnp.sum(lax.all_to_all(slices, NEAR, 0, 0, tiled=True), axis=0)  11.1 us
    pallas_call x2, Pallas kernels, turn_pair(): pl.pallas_call(functools.partial(turn_kernel, first), out_shape=(jax.Shap...  9.71 us
    all_to_all x1, blocking collectives, spread(): return lax.all_to_all(copies, axis, 0, 0, tiled=True)  9.23 us
    pallas_call x1, Pallas kernels, sweep_last(): pl.pallas_call(functools.partial(last_kernel, rows), grid=(own.shape[0] /...  6.83 us
  transfers between devices with their start and end apart: 11, of which 2 were waited for; matrix products, arithmetic and copies ran while one was open for 3% of the time, Pallas kernels for 7%

profile of v4, /device:TPU:2, one launch (start us, length us, event | category | flops | bytes accessed | tf_op | source)
XLA Modules:
  0.0 139.5 jit_solution(5555172211273084535)
XLA Ops:
  0.6 0.0 copy-start
  0.6 1.1 split.11
  1.7 1.3 collective-permute-start.4
  3.0 1.0 split.10
  4.0 1.4 collective-permute-start.3
  5.4 0.0 copy-done
  5.4 0.1 slice.47
  5.4 3.4 %collective-permute-start.1 = (f32[808,256]{1,0:T(8,128)S(1)}, f32[808,256]{1,0:T(8,128)S(1)}, u32[]{:S(2)}, u32[]{:S(2)}) collective-permute-start(f32[808,256]{1,0:T(8,128)S(1)} %slice.47), channel_id=1, source_target_pairs={{0,64},{256,320},{64,128},{320,384},{128,192},{384,448},{192,0},{4... | collective-permute-start | bytes 2482184 | tf_op jit(solution)/shard_map/ppermute | solution.py:26
  8.8 1.0 fusion.7
  9.9 11.1 %all_to_all.30 = f32[8,48,128]{2,1,0:T(8,128)S(1)} all-to-all(f32[8,48,128]{2,1,0:T(8,128)S(1)} %bitcast.12), channel_id=1, replica_groups=mesh['z_hi'=2,'x'=4,'z_lo'=8,'y'=4,'core'=2] {'y','core'}, dimensions={0} | all-to-all | bytes 393216 | tf_op jit(solution)/shard_map/all_to_all | solution.py:60
  21.0 0.0 collective-permute-done.4
  21.0 0.0 collective-permute-done.3
  21.1 0.7 broadcast_in_dim.18
  21.7 12.5 %all-to-all-start.2 = ((f32[8,48,128]{2,1,0:T(8,128)}), f32[8,48,128]{2,1,0:T(8,128)S(1)}, u32[]{:S(2)}, u32[]{:S(2)}) async-start(f32[8,48,128]{2,1,0:T(8,128)} %broadcast_in_dim.18), calls=%async_computation.2 | async-start | bytes 393216 | tf_op jit(solution)/shard_map/all_to_all | solution.py:54
  34.3 0.7 collective-permute-start.5
  34.9 9.5 %collective-permute-start.6 = (f32[272,256]{1,0:T(8,128)}, f32[272,256]{1,0:T(8,128)}, u32[]{:S(2)}, u32[]{:S(2)}) collective-permute-start(f32[272,256]{1,0:T(8,128)} %collective-permute-done.4), channel_id=1, source_target_pairs={{64,256},{320,0},{65,257},{321,1},{66,258},{322,2},{67,259},{323,3... | collective-permute-start | bytes 835592 | tf_op jit(solution)/shard_map/ppermute | solution.py:26
  44.5 0.0 collective-permute-done.1
  44.5 0.0 copy-start.3
  44.5 1.4 collective-permute-start.2
  45.9 2.8 %collective-permute-start = (f32[216,256]{1,0:T(8,128)S(1)}, f32[216,256]{1,0:T(8,128)S(1)}, u32[]{:S(2)}, u32[]{:S(2)}) collective-permute-start(f32[216,256]{1,0:T(8,128)S(1)} %split.9), channel_id=1, source_target_pairs={{0,64},{64,128},{128,192},{192,256},{256,320},{320,384},{384,448},... | collective-permute-start | bytes 663560 | tf_op jit(solution)/shard_map/ppermute | solution.py:26
  48.7 0.0 copy-done.3
  48.7 0.0 all-to-all-done.2
  48.8 21.3 %collective-permute-start.7 = (f32[56,128]{1,0:T(8,128)S(1)}, f32[56,128]{1,0:T(8,128)S(1)}, u32[]{:S(2)}, u32[]{:S(2)}) collective-permute-start(f32[56,128]{1,0:T(8,128)S(1)} %pad_maximum_fusion.3), channel_id=1, source_target_pairs={{0,64},{64,128},{128,192},{192,256},{256,320},{320,384},{384,448},... | collective-permute-start | bytes 86024 | tf_op jit(solution)/shard_map/ppermute | solution.py:26
  70.1 0.5 slice.51
  71.2 14.4 %conditional.1 = ((f32[256,128]{1,0:T(8,128)S(1)}, f32[128,128]{1,0:T(8,128)})) conditional(s32[]{:T(128)} %bitcast.3, () %tuple.18, (f32[48,128]{1,0:T(8,128)S(1)}, s32[1,256]{1,0:T(1,128)S(1)}) %tuple.27), branch_computations={%region_2.0_spmd, %region_3.0_spmd} | conditional | flops 5000000000 | bytes 1014408 | solution.py:225
  71.3 9.2 %all_to_all.29.blocks_ref = f32[8,48,128]{2,1,0:T(8,128)S(1)} all-to-all(f32[8,48,128]{2,1,0:T(8,128)S(1)} %broadcast_in_dim.3), channel_id=1, replica_groups=mesh['z_hi'=2,'x'=4,'z_lo'=8,'y'=4,'core'=2] {'y','core'}, dimensions={0} | all-to-all | bytes 393216 | tf_op jit(solution)/shard_map/cond/branch_1_fun/all_to_all | solution.py:54
  80.5 5.2 %turn_pair.2 = (f32[256,128]{1,0:T(8,128)S(1)}, f32[128,128]{1,0:T(8,128)}) custom-call(f32[8,48,128]{2,1,0:T(8,128)S(1)} %all_to_all.29.blocks_ref, s32[1,256]{1,0:T(1,128)S(1)} %get-tuple-element.5.order_ref), custom_call_target="tpu_custom_call" | custom-call | flops 5000000000 | bytes 400000 | tf_op jit(solution)/shard_map/cond/branch_1_fun/turn_pair/pallas_call | solution.py:148
  85.7 0.0 collective-permute-done
  85.7 0.0 copy-start.1
  85.7 0.0 collective-permute-done.6
  85.7 0.0 collective-permute-done.5
  85.7 0.0 collective-permute-done.7
  85.7 0.0 collective-permute-done.2
  85.7 1.2 maximum_select_fusion
  86.9 0.0 copy-done.1
  86.9 1.0 fusion.5
  88.0 12.1 %all_to_all.31 = f32[8,112,128]{2,1,0:T(8,128)S(1)} all-to-all(f32[8,112,128]{2,1,0:T(8,128)S(1)} %pad_maximum_fusion.1), channel_id=1, replica_groups=mesh['z_hi'=2,'x'=4,'z_lo'=8,'y'=4,'core'=2] {'y','core'}, dimensions={0} | all-to-all | bytes 917504 | tf_op jit(solution)/shard_map/all_to_all | solution.py:243
  100.2 0.1 fusion
  100.3 0.2 convolution_add_fusion
  100.4 0.7 broadcast_in_dim.22
  101.1 8.9 %all-to-all-start.4 = ((f32[8,32,128]{2,1,0:T(8,128)}), f32[8,32,128]{2,1,0:T(8,128)}, u32[]{:S(2)}, u32[]{:S(2)}) async-start(f32[8,32,128]{2,1,0:T(8,128)} %broadcast_in_dim.22), calls=%async_computation.4 | async-start | bytes 262144 | tf_op jit(solution)/shard_map/all_to_all | solution.py:54
  110.0 1.0 pad_maximum_fusion.behind_ref
  111.0 10.6 %all-to-all-done.4 = f32[8,32,128]{2,1,0:T(8,128)} async-done(((f32[8,32,128]{2,1,0:T(8,128)}), f32[8,32,128]{2,1,0:T(8,128)}, u32[]{:S(2)}, u32[]{:S(2)}) %all-to-all-start.4) | async-done | bytes 131104 | tf_op jit(solution)/shard_map/all_to_all | solution.py:54
  121.6 0.9 reduce_sum.39
  122.5 0.7 broadcast_in_dim.23
  123.2 3.6 %all-to-all-start.5 = ((f32[8,32,128]{2,1,0:T(8,128)}), f32[8,32,128]{2,1,0:T(8,128)S(1)}, u32[]{:S(2)}, u32[]{:S(2)}) async-start(f32[8,32,128]{2,1,0:T(8,128)} %broadcast_in_dim.23), calls=%async_computation.5 | async-start | bytes 262144 | tf_op jit(solution)/shard_map/all_to_all | solution.py:54
  126.8 0.0 copy-start.2
  126.8 4.5 %turn_pair.3 = (f32[256,128]{1,0:T(8,128)S(1)}, f32[128,128]{1,0:T(8,128)S(1)}) custom-call(f32[8,48,128]{2,1,0:T(8,128)S(1)} %slice.70.blocks_ref, s32[1,256]{1,0:T(1,128)S(1)} %bitcast.11), custom_call_target="tpu_custom_call" | custom-call | flops 5000000000 | bytes 400000 | tf_op jit(solution)/shard_map/turn_pair/pallas_call | solution.py:148
  131.3 1.3 all-to-all-done.5.cross_ref
  132.6 0.0 copy-done.2
  132.6 6.8 %sweep_last.1 = (f32[1024,256]{1,0:T(8,128)}, f32[1,256]{1,0:T(1,128)}) custom-call(f32[8,32,128]{2,1,0:T(8,128)S(1)} %all-to-all-done.5.cross_ref, f32[256,128]{1,0:T(8,128)S(1)} %get-tuple-element.32.kept_ref, f32[128,128]{1,0:T(8,128)S(1)} %copy-done.2, f32[256,128]{1,0:T(8,128)S(1)} %get-tuple-element.34.given_ref, ...), custom_call_target="tpu_custom_call" | custom-call | tf_op jit(solution)/shard_map/sweep_last/pallas_call | solution.py:184
  (18 shorter events, 0.2 us)
Async XLA Ops:
  0.6 4.8 %copy-start = (f32[1024,256]{1,0:T(8,128)S(1)}, f32[1024,256]{1,0:T(8,128)}, u32[]{:S(2)}) copy-start(f32[1024,256]{1,0:T(8,128)} %own_ref.1) | copy-start | bytes 3145732
  1.7 19.3 %collective-permute-start.4 = (f32[272,256]{1,0:T(8,128)S(1)}, f32[272,256]{1,0:T(8,128)}, u32[]{:S(2)}, u32[]{:S(2)}) collective-permute-start(f32[272,256]{1,0:T(8,128)S(1)} %split.11), channel_id=1, source_target_pairs={{192,64},{448,320},{193,65},{449,321},{194,66},{450,322},{195,67},... | collective-permute-start | bytes 835592 | tf_op jit(solution)/shard_map/ppermute | solution.py:26
  4.0 17.1 %collective-permute-start.3 = (f32[280,256]{1,0:T(8,128)S(1)}, f32[280,256]{1,0:T(8,128)}, u32[]{:S(2)}, u32[]{:S(2)}) collective-permute-start(f32[280,256]{1,0:T(8,128)S(1)} %split.10), channel_id=1, source_target_pairs={{192,128},{448,384},{193,129},{449,385},{194,130},{450,386},{195,1... | collective-permute-start | bytes 860168 | tf_op jit(solution)/shard_map/ppermute | solution.py:26
  5.4 39.0 %collective-permute-start.1 = (f32[808,256]{1,0:T(8,128)S(1)}, f32[808,256]{1,0:T(8,128)S(1)}, u32[]{:S(2)}, u32[]{:S(2)}) collective-permute-start(f32[808,256]{1,0:T(8,128)S(1)} %slice.47), channel_id=1, source_target_pairs={{0,64},{256,320},{64,128},{320,384},{128,192},{384,448},{192,0},{4... | collective-permute-start | bytes 2482184 | tf_op jit(solution)/shard_map/ppermute | solution.py:26
  21.7 27.0 %all-to-all-start.2 = ((f32[8,48,128]{2,1,0:T(8,128)}), f32[8,48,128]{2,1,0:T(8,128)S(1)}, u32[]{:S(2)}, u32[]{:S(2)}) async-start(f32[8,48,128]{2,1,0:T(8,128)} %broadcast_in_dim.18), calls=%async_computation.2 | async-start | bytes 393216 | tf_op jit(solution)/shard_map/all_to_all | solution.py:54
  34.3 51.4 %collective-permute-start.5 = (f32[280,256]{1,0:T(8,128)}, f32[280,256]{1,0:T(8,128)S(1)}, u32[]{:S(2)}, u32[]{:S(2)}) collective-permute-start(f32[280,256]{1,0:T(8,128)} %collective-permute-done.3), channel_id=1, source_target_pairs={{128,256},{384,0},{129,257},{385,1},{130,258},{386,2},{131,259},{3... | collective-permute-start | bytes 860168 | tf_op jit(solution)/shard_map/ppermute | solution.py:26
  34.9 50.7 %collective-permute-start.6 = (f32[272,256]{1,0:T(8,128)}, f32[272,256]{1,0:T(8,128)}, u32[]{:S(2)}, u32[]{:S(2)}) collective-permute-start(f32[272,256]{1,0:T(8,128)} %collective-permute-done.4), channel_id=1, source_target_pairs={{64,256},{320,0},{65,257},{321,1},{66,258},{322,2},{67,259},{323,3... | collective-permute-start | bytes 835592 | tf_op jit(solution)/shard_map/ppermute | solution.py:26
  44.5 4.2 %copy-start.3 = (s32[1,256]{1,0:T(1,128)S(1)}, s32[1,256]{1,0:T(1,128)}, u32[]{:S(2)}) copy-start(s32[1,256]{1,0:T(1,128)} %param.5) | copy-start | bytes 3076
  44.5 41.2 %collective-permute-start.2 = (f32[256,256]{1,0:T(8,128)S(1)}, f32[256,256]{1,0:T(8,128)}, u32[]{:S(2)}, u32[]{:S(2)}) collective-permute-start(f32[256,256]{1,0:T(8,128)S(1)} %slice.62), channel_id=1, source_target_pairs={{0,256},{256,0},{1,257},{257,1},{2,258},{258,2},{3,259},{259,3},{4... | collective-permute-start | bytes 786440 | tf_op jit(solution)/shard_map/ppermute | solution.py:26
  45.9 39.8 %collective-permute-start = (f32[216,256]{1,0:T(8,128)S(1)}, f32[216,256]{1,0:T(8,128)S(1)}, u32[]{:S(2)}, u32[]{:S(2)}) collective-permute-start(f32[216,256]{1,0:T(8,128)S(1)} %split.9), channel_id=1, source_target_pairs={{0,64},{64,128},{128,192},{192,256},{256,320},{320,384},{384,448},... | collective-permute-start | bytes 663560 | tf_op jit(solution)/shard_map/ppermute | solution.py:26
  48.8 37.0 %collective-permute-start.7 = (f32[56,128]{1,0:T(8,128)S(1)}, f32[56,128]{1,0:T(8,128)S(1)}, u32[]{:S(2)}, u32[]{:S(2)}) collective-permute-start(f32[56,128]{1,0:T(8,128)S(1)} %pad_maximum_fusion.3), channel_id=1, source_target_pairs={{0,64},{64,128},{128,192},{192,256},{256,320},{320,384},{384,448},... | collective-permute-start | bytes 86024 | tf_op jit(solution)/shard_map/ppermute | solution.py:26
  85.7 1.2 copy-start.1
  101.1 20.5 %all-to-all-start.4 = ((f32[8,32,128]{2,1,0:T(8,128)}), f32[8,32,128]{2,1,0:T(8,128)}, u32[]{:S(2)}, u32[]{:S(2)}) async-start(f32[8,32,128]{2,1,0:T(8,128)} %broadcast_in_dim.22), calls=%async_computation.4 | async-start | bytes 262144 | tf_op jit(solution)/shard_map/all_to_all | solution.py:54
  123.2 9.4 %all-to-all-start.5 = ((f32[8,32,128]{2,1,0:T(8,128)}), f32[8,32,128]{2,1,0:T(8,128)S(1)}, u32[]{:S(2)}, u32[]{:S(2)}) async-start(f32[8,32,128]{2,1,0:T(8,128)} %broadcast_in_dim.23), calls=%async_computation.5 | async-start | bytes 262144 | tf_op jit(solution)/shard_map/all_to_all | solution.py:54
  126.8 5.9 %copy-start.2 = (f32[128,128]{1,0:T(8,128)S(1)}, f32[128,128]{1,0:T(8,128)}, u32[]{:S(2)}) copy-start(f32[128,128]{1,0:T(8,128)} %get-tuple-element.33.gram_ref) | copy-start | bytes 196612

commit v5 on v4

--- a/solution.py
+++ b/solution.py
@@ -19,7 +19,7 @@
 COL = ("z_hi", "x")
 
 
-DIRECT, RING, TWO, ONE = 216, 256, 280, 272
+DIRECT, RING, TWO, ONE = 272, 224, 264, 264
 
 
 def send(shard, pairs):
@@ -203,9 +203,9 @@
     rows, width = matrix.shape
     half = width // 2
     place = lax.axis_index("x")
-    part, whole = first_blocks(matrix), matrix
-    direct, _, two, one = jnp.split(whole, [DIRECT, DIRECT + RING, DIRECT + RING + TWO])
-    turned = send(whole[DIRECT:], sum([inside(i, (i + 1) % 4) for i in range(4)], []))
+    direct, _, two, one = jnp.split(matrix, [DIRECT, DIRECT + RING, DIRECT + RING + TWO])
+    turned = send(matrix[DIRECT:], sum([inside(i, (i + 1) % 4) for i in range(4)], []))
+    part, two, one = lax.optimization_barrier((first_blocks(matrix), two, one))
     at_two = send(two, inside(3, 2))
     at_one = send(one, inside(3, 1))
     slices = near_sum(part)
@@ -236,18 +236,17 @@
     crossed = jnp.concatenate([crossed_ring, crossed_two, crossed_one], axis=0)
     behind = jnp.concatenate([direct, jnp.where(place == 0, crossed, turned)], axis=0)
     near = lax.axis_size(NEAR)
-    cross = inner_gram(behind, matrix)
     cut = width // near
-    parts = [cross[:, :half].reshape(near, cut, half), cross[:, half:].reshape(near, cut, half)]
-    parts.append(jnp.broadcast_to(arrived[None, :share], (near, share, half)))
+    cross = inner_gram(behind, product(matrix, kept_basis)).reshape(near, cut, half)
+    parts = [cross, jnp.broadcast_to(arrived[None, :share], (near, share, half))]
     parts = lax.all_to_all(jnp.concatenate(parts, axis=1), NEAR, 0, 0, tiled=True)
-    cross = jnp.sum(parts[:, : 2 * cut], axis=0)
-    cross = product(cross[:cut], kept_basis[:half]) + product(cross[cut:], kept_basis[half:])
+    cross = far_sum(jnp.sum(parts[:, :cut], axis=0))
     behind_keep = arrived[share : share + 2].reshape(1, width).astype(jnp.int32)
-    given_basis, given_gram = turn_pair(parts[:, 2 * cut :], behind_keep, half)
+    given_basis, given_gram = turn_pair(parts[:, cut:], behind_keep, half)
+    cross, given_basis, given_gram = lax.optimization_barrier((cross, given_basis, given_gram))
     rotated, norms = sweep_last(
         rows * lax.axis_size(ROW),
-        spread(far_sum(cross), NEAR),
+        spread(cross, NEAR),
         kept_basis,
         kept_gram,
         given_basis,

time: 140 us -> 137 us (0.979)
  the two profiles are of different devices: /device:TPU:2 before, /device:TPU:1 now
where the time goes in v5:
time: 137 us; the launch traced here: 134 us
  starting transfers between devices  66.2 us (48%)
  waiting for transfers between devices  21 us (15%)
  blocking collectives  17.3 us (13%)
  Pallas kernels  15.9 us (12%)
  matrix products  5.27 us (4%)
  other arithmetic  3.73 us (3%)
  local copies, waits for them, and re-layouts  3.32 us (2%)
  between operations  1.61 us (1%)
    ppermute x8, starting transfers between devices, send(): return lax.ppermute(shard, COL, pairs)  27.8 us
    all_to_all x3, starting transfers between devices, spread(): return lax.all_to_all(copies, axis, 0, 0, tiled=True)  21.2 us
    all_to_all x1, blocking collectives, spread(): return lax.all_to_all(copies, axis, 0, 0, tiled=True)  17.3 us
    all_to_all x1, starting transfers between devices, near_sum(): return jnp.sum(lax.all_to_all(slices, NEAR, 0, 0, tiled=True), axis=0)  10.2 us
    all_to_all x3, waiting for transfers between devices, spread(): return lax.all_to_all(copies, axis, 0, 0, tiled=True)  9.99 us
    pallas_call x2, Pallas kernels, turn_pair(): pl.pallas_call(functools.partial(turn_kernel, first), out_shape=(jax.Shap...  9.07 us
    all_to_all x1, waiting for transfers between devices, shards(): lax.all_to_all(jnp.concatenate(parts, axis=1), NEAR, 0, 0, tiled=True)  7.11 us
    all_to_all x1, starting transfers between devices, shards(): lax.all_to_all(jnp.concatenate(parts, axis=1), NEAR, 0, 0, tiled=True)  7.05 us
  transfers between devices with their start and end apart: 13, of which 4 were waited for; matrix products, arithmetic and copies ran while one was open for 2% of the time, Pallas kernels for 7%

profile of v5, /device:TPU:1, one launch (start us, length us, event | category | flops | bytes accessed | tf_op | source)
XLA Modules:
  0.0 134.3 jit_solution(15592876882496401184)
XLA Ops:
  0.6 0.0 copy-start
  0.6 2.6 %fusion.2 = f32[256,256]{1,0:T(8,128)S(1)} fusion(f32[1024,256]{1,0:T(8,128)} %own_ref.1), kind=kOutput, calls=%fused_computation.9 | convolution fusion | flops 402653184 | bytes 1310720 | tf_op jit(solution)/shard_map/dot_general | solution.py:42
  3.3 0.0 copy-done
  3.4 0.7 pad_maximum_fusion.2
  4.1 1.4 %collective-permute-start.3 = (f32[264,256]{1,0:T(8,128)S(1)}, f32[264,256]{1,0:T(8,128)}, u32[]{:S(2)}, u32[]{:S(2)}) collective-permute-start(f32[264,256]{1,0:T(8,128)S(1)} %get-tuple-element.29), channel_id=1, source_target_pairs={{192,128},{448,384},{193,129},{449,385},{194,130},{450,386},{195,1... | collective-permute-start | bytes 811016 | tf_op jit(solution)/shard_map/ppermute | solution.py:26
  5.4 1.4 %collective-permute-start.4 = (f32[264,256]{1,0:T(8,128)S(1)}, f32[264,256]{1,0:T(8,128)}, u32[]{:S(2)}, u32[]{:S(2)}) collective-permute-start(f32[264,256]{1,0:T(8,128)S(1)} %get-tuple-element.30), channel_id=1, source_target_pairs={{192,64},{448,320},{193,65},{449,321},{194,66},{450,322},{195,67},... | collective-permute-start | bytes 811016 | tf_op jit(solution)/shard_map/ppermute | solution.py:26
  6.8 10.2 %all-to-all-start.1 = ((f32[8,48,128]{2,1,0:T(8,128)}), f32[8,48,128]{2,1,0:T(8,128)S(1)}, u32[]{:S(2)}, u32[]{:S(2)}) async-start(f32[8,48,128]{2,1,0:T(8,128)} %bitcast), calls=%async_computation.1 | async-start | bytes 393216 | tf_op jit(solution)/shard_map/all_to_all | solution.py:60
  16.9 0.1 slice.29
  17.0 1.9 %collective-permute-start.1 = (f32[752,256]{1,0:T(8,128)S(1)}, f32[752,256]{1,0:T(8,128)S(1)}, u32[]{:S(2)}, u32[]{:S(2)}) collective-permute-start(f32[752,256]{1,0:T(8,128)S(1)} %slice.29), channel_id=1, source_target_pairs={{0,64},{256,320},{64,128},{320,384},{128,192},{384,448},{192,0},{4... | collective-permute-start | bytes 2310152 | tf_op jit(solution)/shard_map/ppermute | solution.py:26
  18.9 3.9 %all-to-all-done.1 = f32[8,48,128]{2,1,0:T(8,128)S(1)} async-done(((f32[8,48,128]{2,1,0:T(8,128)}), f32[8,48,128]{2,1,0:T(8,128)S(1)}, u32[]{:S(2)}, u32[]{:S(2)}) %all-to-all-start.1) | async-done | bytes 196640 | tf_op jit(solution)/shard_map/all_to_all | solution.py:60
  22.9 0.0 collective-permute-done.3
  22.9 0.0 collective-permute-done.4
  22.9 0.7 broadcast_in_dim.18
  23.6 8.0 %all-to-all-start.2 = ((f32[8,48,128]{2,1,0:T(8,128)}), f32[8,48,128]{2,1,0:T(8,128)S(1)}, u32[]{:S(2)}, u32[]{:S(2)}) async-start(f32[8,48,128]{2,1,0:T(8,128)} %broadcast_in_dim.18), calls=%async_computation.2 | async-start | bytes 393216 | tf_op jit(solution)/shard_map/all_to_all | solution.py:54
  31.6 0.0 copy-start.3
  31.6 5.4 %collective-permute-start = (f32[272,256]{1,0:T(8,128)S(1)}, f32[272,256]{1,0:T(8,128)}, u32[]{:S(2)}, u32[]{:S(2)}) collective-permute-start(f32[272,256]{1,0:T(8,128)S(1)} %split.9), channel_id=1, source_target_pairs={{0,64},{64,128},{128,192},{192,256},{256,320},{320,384},{384,448},... | collective-permute-start | bytes 835592 | tf_op jit(solution)/shard_map/ppermute | solution.py:26
  37.0 1.3 collective-permute-start.5
  38.3 1.3 collective-permute-start.6
  39.6 0.0 collective-permute-done.1
  39.7 13.2 %collective-permute-start.2 = (f32[224,256]{1,0:T(8,128)S(1)}, f32[224,256]{1,0:T(8,128)}, u32[]{:S(2)}, u32[]{:S(2)}) collective-permute-start(f32[224,256]{1,0:T(8,128)S(1)} %slice.38), channel_id=1, source_target_pairs={{0,256},{256,0},{1,257},{257,1},{2,258},{258,2},{3,259},{259,3},{4... | collective-permute-start | bytes 688136 | tf_op jit(solution)/shard_map/ppermute | solution.py:26
  52.9 0.0 copy-done.3
  52.9 0.0 all-to-all-done.2
  53.0 1.9 %collective-permute-start.7 = (f32[56,128]{1,0:T(8,128)S(1)}, f32[56,128]{1,0:T(8,128)S(1)}, u32[]{:S(2)}, u32[]{:S(2)}) collective-permute-start(f32[56,128]{1,0:T(8,128)S(1)} %pad_maximum_fusion.3), channel_id=1, source_target_pairs={{0,64},{64,128},{128,192},{192,256},{256,320},{320,384},{384,448},... | collective-permute-start | bytes 86024 | tf_op jit(solution)/shard_map/ppermute | solution.py:26
  54.9 0.5 slice.33
  56.1 21.8 %conditional.1 = ((f32[256,128]{1,0:T(8,128)S(1)}, f32[128,128]{1,0:T(8,128)S(1)})) conditional(s32[]{:T(128)} %bitcast.3, () %tuple.21, (f32[48,128]{1,0:T(8,128)S(1)}, s32[1,256]{1,0:T(1,128)S(1)}) %tuple.31), branch_computations={%region_2.0_spmd, %region_3.0_spmd} | conditional | flops 5000000000 | bytes 1014408 | solution.py:225
  56.1 17.3 %all_to_all.29.blocks_ref = f32[8,48,128]{2,1,0:T(8,128)S(1)} all-to-all(f32[8,48,128]{2,1,0:T(8,128)S(1)} %broadcast_in_dim.3), channel_id=1, replica_groups=mesh['z_hi'=2,'x'=4,'z_lo'=8,'y'=4,'core'=2] {'y','core'}, dimensions={0} | all-to-all | bytes 393216 | tf_op jit(solution)/shard_map/cond/branch_1_fun/all_to_all | solution.py:54
  73.4 4.5 %turn_pair.2 = (f32[256,128]{1,0:T(8,128)S(1)}, f32[128,128]{1,0:T(8,128)S(1)}) custom-call(f32[8,48,128]{2,1,0:T(8,128)S(1)} %all_to_all.29.blocks_ref, s32[1,256]{1,0:T(1,128)S(1)} %get-tuple-element.5.order_ref), custom_call_target="tpu_custom_call" | custom-call | flops 5000000000 | bytes 400000 | tf_op jit(solution)/shard_map/cond/branch_1_fun/turn_pair/pallas_call | solution.py:148
  77.9 0.0 collective-permute-done
  77.9 0.0 collective-permute-done.5
  78.0 0.0 collective-permute-done.6
  78.0 0.0 collective-permute-done.7
  78.0 0.0 copy-start.1
  78.0 0.0 collective-permute-done.2
  78.0 0.6 copy-done.1
  78.6 0.7 fusion.3
  79.3 1.2 maximum_select_fusion
  80.5 0.0 slice-start
  80.5 2.0 %fusion = f32[256,128]{1,0:T(8,128)S(1)} fusion(f32[128,1024]{1,0:T(8,128)S(1)} %fusion.3, f32[752,256]{1,0:T(8,128)S(1)} %maximum_select_fusion, f32[272,256]{1,0:T(8,128)} %collective-permute-done), kind=kOutput, calls=%fused_computation.7 | convolution fusion | flops 201588736 | bytes 1703936 | tf_op jit(solution)/shard_map/dot_general | solution.py:42
  82.5 0.0 slice-done
  82.5 0.7 pad_maximum_fusion.1
  83.2 0.0 copy-start.2
  83.2 7.0 %all-to-all-start.3 = ((f32[8,80,128]{2,1,0:T(8,128)}), f32[8,80,128]{2,1,0:T(8,128)S(1)}, u32[]{:S(2)}, u32[]{:S(2)}) async-start(f32[8,80,128]{2,1,0:T(8,128)} %pad_maximum_fusion.1), calls=%async_computation.3 | async-start | bytes 655360 | tf_op jit(solution)/shard_map/all_to_all | solution.py:242
  90.3 0.0 copy-done.2
  90.3 7.1 %all-to-all-done.3 = f32[8,80,128]{2,1,0:T(8,128)S(1)} async-done(((f32[8,80,128]{2,1,0:T(8,128)}), f32[8,80,128]{2,1,0:T(8,128)S(1)}, u32[]{:S(2)}, u32[]{:S(2)}) %all-to-all-start.3) | async-done | bytes 327712 | tf_op jit(solution)/shard_map/all_to_all | solution.py:242
  97.4 0.7 broadcast_in_dim.22
  98.1 7.2 %all-to-all-start.4 = ((f32[8,32,128]{2,1,0:T(8,128)}), f32[8,32,128]{2,1,0:T(8,128)S(1)}, u32[]{:S(2)}, u32[]{:S(2)}) async-start(f32[8,32,128]{2,1,0:T(8,128)} %broadcast_in_dim.22), calls=%async_computation.4 | async-start | bytes 262144 | tf_op jit(solution)/shard_map/all_to_all | solution.py:54
  105.3 4.5 %turn_pair.3 = (f32[256,128]{1,0:T(8,128)S(1)}, f32[128,128]{1,0:T(8,128)S(1)}) custom-call(f32[8,48,128]{2,1,0:T(8,128)S(1)} %slice.42.blocks_ref, s32[1,256]{1,0:T(1,128)S(1)} %bitcast.12), custom_call_target="tpu_custom_call" | custom-call | flops 5000000000 | bytes 400000 | tf_op jit(solution)/shard_map/turn_pair/pallas_call | solution.py:148
  109.9 5.7 %all-to-all-done.4 = f32[8,32,128]{2,1,0:T(8,128)S(1)} async-done(((f32[8,32,128]{2,1,0:T(8,128)}), f32[8,32,128]{2,1,0:T(8,128)S(1)}, u32[]{:S(2)}, u32[]{:S(2)}) %all-to-all-start.4) | async-done | bytes 131104 | tf_op jit(solution)/shard_map/all_to_all | solution.py:54
  115.6 0.7 broadcast_in_dim.23
  116.3 5.9 %all-to-all-start.5 = ((f32[8,32,128]{2,1,0:T(8,128)}), f32[8,32,128]{2,1,0:T(8,128)S(1)}, u32[]{:S(2)}, u32[]{:S(2)}) async-start(f32[8,32,128]{2,1,0:T(8,128)} %broadcast_in_dim.23), calls=%async_computation.5 | async-start | bytes 262144 | tf_op jit(solution)/shard_map/all_to_all | solution.py:54
  122.2 1.0 pad_maximum_fusion.behind_ref
  123.2 4.3 %all-to-all-done.5.cross_ref = f32[8,32,128]{2,1,0:T(8,128)S(1)} async-done(((f32[8,32,128]{2,1,0:T(8,128)}), f32[8,32,128]{2,1,0:T(8,128)S(1)}, u32[]{:S(2)}, u32[]{:S(2)}) %all-to-all-start.5) | async-done | bytes 131104 | tf_op jit(solution)/shard_map/all_to_all | solution.py:54
  127.5 6.8 %sweep_last.1 = (f32[1024,256]{1,0:T(8,128)}, f32[1,256]{1,0:T(1,128)}) custom-call(f32[8,32,128]{2,1,0:T(8,128)S(1)} %all-to-all-done.5.cross_ref, f32[256,128]{1,0:T(8,128)S(1)} %get-tuple-element.40.kept_ref, f32[128,128]{1,0:T(8,128)S(1)} %get-tuple-element.45.gram_ref, f32[256,128]{1,0:T(8,128)S(1)} %get-tuple-element.46.given_ref, ...), custom_call_target="tpu_custom_call" | custom-call | tf_op jit(solution)/shard_map/sweep_last/pallas_call | solution.py:184
  (16 shorter events, 0.2 us)
Async XLA Ops:
  0.6 2.7 %copy-start = (f32[1024,256]{1,0:T(8,128)S(1)}, f32[1024,256]{1,0:T(8,128)}, u32[]{:S(2)}) copy-start(f32[1024,256]{1,0:T(8,128)} %own_ref.1) | copy-start | bytes 3145732
  4.1 18.8 %collective-permute-start.3 = (f32[264,256]{1,0:T(8,128)S(1)}, f32[264,256]{1,0:T(8,128)}, u32[]{:S(2)}, u32[]{:S(2)}) collective-permute-start(f32[264,256]{1,0:T(8,128)S(1)} %get-tuple-element.29), channel_id=1, source_target_pairs={{192,128},{448,384},{193,129},{449,385},{194,130},{450,386},{195,1... | collective-permute-start | bytes 811016 | tf_op jit(solution)/shard_map/ppermute | solution.py:26
  5.4 17.5 %collective-permute-start.4 = (f32[264,256]{1,0:T(8,128)S(1)}, f32[264,256]{1,0:T(8,128)}, u32[]{:S(2)}, u32[]{:S(2)}) collective-permute-start(f32[264,256]{1,0:T(8,128)S(1)} %get-tuple-element.30), channel_id=1, source_target_pairs={{192,64},{448,320},{193,65},{449,321},{194,66},{450,322},{195,67},... | collective-permute-start | bytes 811016 | tf_op jit(solution)/shard_map/ppermute | solution.py:26
  6.8 16.1 %all-to-all-start.1 = ((f32[8,48,128]{2,1,0:T(8,128)}), f32[8,48,128]{2,1,0:T(8,128)S(1)}, u32[]{:S(2)}, u32[]{:S(2)}) async-start(f32[8,48,128]{2,1,0:T(8,128)} %bitcast), calls=%async_computation.1 | async-start | bytes 393216 | tf_op jit(solution)/shard_map/all_to_all | solution.py:60
  17.0 22.6 %collective-permute-start.1 = (f32[752,256]{1,0:T(8,128)S(1)}, f32[752,256]{1,0:T(8,128)S(1)}, u32[]{:S(2)}, u32[]{:S(2)}) collective-permute-start(f32[752,256]{1,0:T(8,128)S(1)} %slice.29), channel_id=1, source_target_pairs={{0,64},{256,320},{64,128},{320,384},{128,192},{384,448},{192,0},{4... | collective-permute-start | bytes 2310152 | tf_op jit(solution)/shard_map/ppermute | solution.py:26
  23.6 29.4 %all-to-all-start.2 = ((f32[8,48,128]{2,1,0:T(8,128)}), f32[8,48,128]{2,1,0:T(8,128)S(1)}, u32[]{:S(2)}, u32[]{:S(2)}) async-start(f32[8,48,128]{2,1,0:T(8,128)} %broadcast_in_dim.18), calls=%async_computation.2 | async-start | bytes 393216 | tf_op jit(solution)/shard_map/all_to_all | solution.py:54
  31.6 21.3 %copy-start.3 = (s32[1,256]{1,0:T(1,128)S(1)}, s32[1,256]{1,0:T(1,128)}, u32[]{:S(2)}) copy-start(s32[1,256]{1,0:T(1,128)} %param.5) | copy-start | bytes 3076
  31.6 46.3 %collective-permute-start = (f32[272,256]{1,0:T(8,128)S(1)}, f32[272,256]{1,0:T(8,128)}, u32[]{:S(2)}, u32[]{:S(2)}) collective-permute-start(f32[272,256]{1,0:T(8,128)S(1)} %split.9), channel_id=1, source_target_pairs={{0,64},{64,128},{128,192},{192,256},{256,320},{320,384},{384,448},... | collective-permute-start | bytes 835592 | tf_op jit(solution)/shard_map/ppermute | solution.py:26
  37.0 40.9 %collective-permute-start.5 = (f32[264,256]{1,0:T(8,128)}, f32[264,256]{1,0:T(8,128)}, u32[]{:S(2)}, u32[]{:S(2)}) collective-permute-start(f32[264,256]{1,0:T(8,128)} %collective-permute-done.3), channel_id=1, source_target_pairs={{128,256},{384,0},{129,257},{385,1},{130,258},{386,2},{131,259},{3... | collective-permute-start | bytes 811016 | tf_op jit(solution)/shard_map/ppermute | solution.py:26
  38.3 39.6 %collective-permute-start.6 = (f32[264,256]{1,0:T(8,128)}, f32[264,256]{1,0:T(8,128)}, u32[]{:S(2)}, u32[]{:S(2)}) collective-permute-start(f32[264,256]{1,0:T(8,128)} %collective-permute-done.4), channel_id=1, source_target_pairs={{64,256},{320,0},{65,257},{321,1},{66,258},{322,2},{67,259},{323,3... | collective-permute-start | bytes 811016 | tf_op jit(solution)/shard_map/ppermute | solution.py:26
  39.7 38.3 %collective-permute-start.2 = (f32[224,256]{1,0:T(8,128)S(1)}, f32[224,256]{1,0:T(8,128)}, u32[]{:S(2)}, u32[]{:S(2)}) collective-permute-start(f32[224,256]{1,0:T(8,128)S(1)} %slice.38), channel_id=1, source_target_pairs={{0,256},{256,0},{1,257},{257,1},{2,258},{258,2},{3,259},{259,3},{4... | collective-permute-start | bytes 688136 | tf_op jit(solution)/shard_map/ppermute | solution.py:26
  53.0 25.0 %collective-permute-start.7 = (f32[56,128]{1,0:T(8,128)S(1)}, f32[56,128]{1,0:T(8,128)S(1)}, u32[]{:S(2)}, u32[]{:S(2)}) collective-permute-start(f32[56,128]{1,0:T(8,128)S(1)} %pad_maximum_fusion.3), channel_id=1, source_target_pairs={{0,64},{64,128},{128,192},{192,256},{256,320},{320,384},{384,448},... | collective-permute-start | bytes 86024 | tf_op jit(solution)/shard_map/ppermute | solution.py:26
  78.0 0.6 copy-start.1
  80.5 2.0 %slice-start = ((f32[56,128]{1,0:T(8,128)}), f32[48,128]{1,0:T(8,128)S(1)}, s32[]{:S(2)}) async-start(f32[56,128]{1,0:T(8,128)} %copy-done.1), calls=%async_computation.6 | async-start | bytes 49152 | tf_op jit(solution)/shard_map/slice | solution.py:241
  83.2 7.1 %copy-start.2 = (f32[56,128]{1,0:T(8,128)S(1)}, f32[56,128]{1,0:T(8,128)}, u32[]{:S(2)}) copy-start(f32[56,128]{1,0:T(8,128)} %copy-done.1) | copy-start | bytes 86020
  83.2 14.2 %all-to-all-start.3 = ((f32[8,80,128]{2,1,0:T(8,128)}), f32[8,80,128]{2,1,0:T(8,128)S(1)}, u32[]{:S(2)}, u32[]{:S(2)}) async-start(f32[8,80,128]{2,1,0:T(8,128)} %pad_maximum_fusion.1), calls=%async_computation.3 | async-start | bytes 655360 | tf_op jit(solution)/shard_map/all_to_all | solution.py:242
  98.1 17.5 %all-to-all-start.4 = ((f32[8,32,128]{2,1,0:T(8,128)}), f32[8,32,128]{2,1,0:T(8,128)S(1)}, u32[]{:S(2)}, u32[]{:S(2)}) async-start(f32[8,32,128]{2,1,0:T(8,128)} %broadcast_in_dim.22), calls=%async_computation.4 | async-start | bytes 262144 | tf_op jit(solution)/shard_map/all_to_all | solution.py:54
  116.3 11.2 %all-to-all-start.5 = ((f32[8,32,128]{2,1,0:T(8,128)}), f32[8,32,128]{2,1,0:T(8,128)S(1)}, u32[]{:S(2)}, u32[]{:S(2)}) async-start(f32[8,32,128]{2,1,0:T(8,128)} %broadcast_in_dim.23), calls=%async_computation.5 | async-start | bytes 262144 | tf_op jit(solution)/shard_map/all_to_all | solution.py:54

commit v6 on v5

--- a/solution.py
+++ b/solution.py
@@ -157,40 +157,41 @@
     )(blocks, order)
 
 
-def last_kernel(rows, cross_ref, kept_ref, gram_ref, given_ref, given_gram_ref, own_ref, behind_ref,
-                out_ref, norm_ref, own_high, own_low, behind_high, behind_low):
+def last_kernel(rows, cross_ref, gram_ref, given_basis_ref, given_gram_ref, kept_ref, given_ref,
+                out_ref, norm_ref, high, low):
     half = kept_ref.shape[1]
 
     @pl.when(pl.program_id(0) == 0)
     def _():
-        given = halves(given_ref[...])
-        between = times(halves(cross_ref[...].reshape(2 * half, half)), given, DOWN)
+        between = times(halves(cross_ref[...].reshape(2 * half, half)), halves(given_basis_ref[...]), DOWN)
         basis, squares = swept(whole_gram(gram_ref[...], between, given_gram_ref[...]), False)
         norm_ref[...] = jnp.sqrt(jnp.maximum(squares, 0.0) / rows + EPSILON)
-        own_high[...], own_low[...] = halves(times(halves(kept_ref[...]), halves(basis[:half])))
-        behind_high[...], behind_low[...] = halves(times(given, halves(basis[half:])))
-
-    out_ref[...] = times(halves(own_ref[...]), (own_high[...], own_low[...])) + times(
-        halves(behind_ref[...]), (behind_high[...], behind_low[...])
-    )
-
-
-def sweep_last(rows, cross, kept, gram, given, given_gram, own, behind):
-    width = own.shape[1]
+        high[...], low[...] = halves(basis)
+
+    pair = jnp.concatenate([kept_ref[...], given_ref[...]], axis=1)
+    out_ref[...] = times(halves(pair), (high[...], low[...]))
+
+
+def sweep_last(rows, cross, gram, given_basis, given_gram, kept, given):
+    half = kept.shape[1]
+    width = 2 * half
     tile = 256
     full = lambda value: pl.BlockSpec(value.shape, lambda step: (0,) * value.ndim)
-    tiles = pl.BlockSpec((tile, width), lambda step: (step, 0))
-    small = (cross, kept, gram, given, given_gram)
+    tiles = lambda size: pl.BlockSpec((tile, size), lambda step: (step, 0))
+    small = (cross, gram, given_basis, given_gram)
     return pl.pallas_call(
         functools.partial(last_kernel, rows),
-        grid=(own.shape[0] // tile,),
-        in_specs=[full(value) for value in small] + [tiles, tiles],
-        out_specs=(tiles, pl.BlockSpec((1, width), lambda step: (0, 0))),
-        out_shape=(jax.ShapeDtypeStruct(own.shape, jnp.float32), jax.ShapeDtypeStruct((1, width), jnp.float32)),
-        scratch_shapes=[pltpu.VMEM((width, width), jnp.bfloat16)] * 4,
+        grid=(kept.shape[0] // tile,),
+        in_specs=[full(value) for value in small] + [tiles(half), tiles(half)],
+        out_specs=(tiles(width), pl.BlockSpec((1, width), lambda step: (0, 0))),
+        out_shape=(
+            jax.ShapeDtypeStruct((kept.shape[0], width), jnp.float32),
+            jax.ShapeDtypeStruct((1, width), jnp.float32),
+        ),
+        scratch_shapes=[pltpu.VMEM((width, width), jnp.bfloat16)] * 2,
         compiler_params=pltpu.CompilerParams(vmem_limit_bytes=40 * 2**20),
         name="sweep_last",
-    )(*small, own, behind)
+    )(*small, kept, given)
 
 
 def first_blocks(matrix):
@@ -237,7 +238,8 @@
     behind = jnp.concatenate([direct, jnp.where(place == 0, crossed, turned)], axis=0)
     near = lax.axis_size(NEAR)
     cut = width // near
-    cross = inner_gram(behind, product(matrix, kept_basis)).reshape(near, cut, half)
+    kept = product(matrix, kept_basis)
+    cross = inner_gram(behind, kept).reshape(near, cut, half)
     parts = [cross, jnp.broadcast_to(arrived[None, :share], (near, share, half))]
     parts = lax.all_to_all(jnp.concatenate(parts, axis=1), NEAR, 0, 0, tiled=True)
     cross = far_sum(jnp.sum(parts[:, :cut], axis=0))
@@ -247,12 +249,11 @@
     rotated, norms = sweep_last(
         rows * lax.axis_size(ROW),
         spread(cross, NEAR),
-        kept_basis,
         kept_gram,
         given_basis,
         given_gram,
-        matrix,
-        behind,
+        kept,
+        product(behind, given_basis),
     )
     return (rotated, norms.reshape(width))
 

time: 137 us -> 136 us (level)
  the two profiles are of different devices: /device:TPU:1 before, /device:TPU:4 now
where the time goes in v6:
time: 136 us; the launch traced here: 135 us
  starting transfers between devices  76 us (56%)
  waiting for transfers between devices  21.1 us (16%)
  Pallas kernels  15.3 us (11%)
  blocking collectives  9.23 us (7%)
  matrix products  4.89 us (4%)
  local copies, waits for them, and re-layouts  3.88 us (3%)
  other arithmetic  2.64 us (2%)
  between operations  1.64 us (1%)
    ppermute x8, starting transfers between devices, send(): return lax.ppermute(shard, COL, pairs)  43.2 us
    all_to_all x3, starting transfers between devices, spread(): return lax.all_to_all(copies, axis, 0, 0, tiled=True)  24.9 us
    all_to_all x3, waiting for transfers between devices, spread(): return lax.all_to_all(copies, axis, 0, 0, tiled=True)  12.2 us
    all_to_all x1, blocking collectives, spread(): return lax.all_to_all(copies, axis, 0, 0, tiled=True)  9.23 us
    pallas_call x2, Pallas kernels, turn_pair(): pl.pallas_call(functools.partial(turn_kernel, first), out_shape=(jax.Shap...  9.07 us
    all_to_all x1, waiting for transfers between devices, shards(): lax.all_to_all(jnp.concatenate(parts, axis=1), NEAR, 0, 0, tiled=True)  7.95 us
    pallas_call x1, Pallas kernels, sweep_last(): pl.pallas_call(functools.partial(last_kernel, rows), grid=(kept.shape[0]...  6.21 us
    all_to_all x1, starting transfers between devices, near_sum(): return jnp.sum(lax.all_to_all(slices, NEAR, 0, 0, tiled=True), axis=0)  4.47 us
  transfers between devices with their start and end apart: 13, of which 4 were waited for; matrix products, arithmetic and copies ran while one was open for 2% of the time, Pallas kernels for 7%

profile of v6, /device:TPU:4, one launch (start us, length us, event | category | flops | bytes accessed | tf_op | source)
XLA Modules:
  0.0 134.7 jit_solution(11706835485888188665)
XLA Ops:
  0.6 0.0 copy-start
  0.6 2.6 %fusion.5 = f32[256,256]{1,0:T(8,128)S(1)} fusion(f32[1024,256]{1,0:T(8,128)} %param.4), kind=kOutput, calls=%fused_computation.12 | convolution fusion | flops 402653184 | bytes 1310720 | tf_op jit(solution)/shard_map/dot_general | solution.py:42
  3.3 0.0 copy-done
  3.4 0.7 pad_maximum_fusion.4
  4.1 1.3 collective-permute-start.3
  5.3 1.4 %collective-permute-start.4 = (f32[264,256]{1,0:T(8,128)S(1)}, f32[264,256]{1,0:T(8,128)}, u32[]{:S(2)}, u32[]{:S(2)}) collective-permute-start(f32[264,256]{1,0:T(8,128)S(1)} %get-tuple-element.30), channel_id=1, source_target_pairs={{192,64},{448,320},{193,65},{449,321},{194,66},{450,322},{195,67},... | collective-permute-start | bytes 811016 | tf_op jit(solution)/shard_map/ppermute | solution.py:26
  6.7 4.5 %all-to-all-start.1 = ((f32[8,48,128]{2,1,0:T(8,128)}), f32[8,48,128]{2,1,0:T(8,128)S(1)}, u32[]{:S(2)}, u32[]{:S(2)}) async-start(f32[8,48,128]{2,1,0:T(8,128)} %bitcast), calls=%async_computation.1 | async-start | bytes 393216 | tf_op jit(solution)/shard_map/all_to_all | solution.py:60
  11.2 0.1 slice.29
  11.2 5.9 %collective-permute-start.1 = (f32[752,256]{1,0:T(8,128)S(1)}, f32[752,256]{1,0:T(8,128)S(1)}, u32[]{:S(2)}, u32[]{:S(2)}) collective-permute-start(f32[752,256]{1,0:T(8,128)S(1)} %slice.29), channel_id=1, source_target_pairs={{0,64},{256,320},{64,128},{320,384},{128,192},{384,448},{192,0},{4... | collective-permute-start | bytes 2310152 | tf_op jit(solution)/shard_map/ppermute | solution.py:26
  17.1 0.9 all-to-all-done.1
  18.0 0.0 collective-permute-done.3
  18.0 0.0 collective-permute-done.4
  18.1 0.7 broadcast_in_dim.18
  18.7 12.5 %all-to-all-start.2 = ((f32[8,48,128]{2,1,0:T(8,128)}), f32[8,48,128]{2,1,0:T(8,128)S(1)}, u32[]{:S(2)}, u32[]{:S(2)}) async-start(f32[8,48,128]{2,1,0:T(8,128)} %broadcast_in_dim.18), calls=%async_computation.2 | async-start | bytes 393216 | tf_op jit(solution)/shard_map/all_to_all | solution.py:54
  31.3 0.0 copy-start.5
  31.3 5.9 %collective-permute-start = (f32[272,256]{1,0:T(8,128)S(1)}, f32[272,256]{1,0:T(8,128)S(1)}, u32[]{:S(2)}, u32[]{:S(2)}) collective-permute-start(f32[272,256]{1,0:T(8,128)S(1)} %split.9), channel_id=1, source_target_pairs={{0,64},{64,128},{128,192},{192,256},{256,320},{320,384},{384,448},... | collective-permute-start | bytes 835592 | tf_op jit(solution)/shard_map/ppermute | solution.py:26
  37.2 9.3 %collective-permute-start.5 = (f32[264,256]{1,0:T(8,128)}, f32[264,256]{1,0:T(8,128)}, u32[]{:S(2)}, u32[]{:S(2)}) collective-permute-start(f32[264,256]{1,0:T(8,128)} %collective-permute-done.3), channel_id=1, source_target_pairs={{128,256},{384,0},{129,257},{385,1},{130,258},{386,2},{131,259},{3... | collective-permute-start | bytes 811016 | tf_op jit(solution)/shard_map/ppermute | solution.py:26
  46.5 1.4 %collective-permute-start.6 = (f32[264,256]{1,0:T(8,128)}, f32[264,256]{1,0:T(8,128)}, u32[]{:S(2)}, u32[]{:S(2)}) collective-permute-start(f32[264,256]{1,0:T(8,128)} %collective-permute-done.4), channel_id=1, source_target_pairs={{64,256},{320,0},{65,257},{321,1},{66,258},{322,2},{67,259},{323,3... | collective-permute-start | bytes 811016 | tf_op jit(solution)/shard_map/ppermute | solution.py:26
  47.9 0.0 collective-permute-done.1
  47.9 0.7 collective-permute-start.2
  48.6 0.0 copy-done.5
  48.6 0.0 all-to-all-done.2
  48.7 17.5 %collective-permute-start.7 = (f32[56,128]{1,0:T(8,128)S(1)}, f32[56,128]{1,0:T(8,128)S(1)}, u32[]{:S(2)}, u32[]{:S(2)}) collective-permute-start(f32[56,128]{1,0:T(8,128)S(1)} %pad_maximum_fusion.5), channel_id=1, source_target_pairs={{0,64},{64,128},{128,192},{192,256},{256,320},{320,384},{384,448},... | collective-permute-start | bytes 86024 | tf_op jit(solution)/shard_map/ppermute | solution.py:26
  66.1 0.5 slice.33
  67.3 13.8 %conditional.1 = ((f32[256,128]{1,0:T(8,128)S(1)}, f32[128,128]{1,0:T(8,128)S(1)})) conditional(s32[]{:T(128)} %bitcast.3, () %tuple.21, (f32[48,128]{1,0:T(8,128)S(1)}, s32[1,256]{1,0:T(1,128)S(1)}) %tuple.31), branch_computations={%region_2.0_spmd, %region_3.0_spmd} | conditional | flops 5000000000 | bytes 1014408 | solution.py:226
  67.3 9.2 %all_to_all.29.blocks_ref = f32[8,48,128]{2,1,0:T(8,128)S(1)} all-to-all(f32[8,48,128]{2,1,0:T(8,128)S(1)} %broadcast_in_dim.3), channel_id=1, replica_groups=mesh['z_hi'=2,'x'=4,'z_lo'=8,'y'=4,'core'=2] {'y','core'}, dimensions={0} | all-to-all | bytes 393216 | tf_op jit(solution)/shard_map/cond/branch_1_fun/all_to_all | solution.py:54
  76.6 4.5 %turn_pair.2 = (f32[256,128]{1,0:T(8,128)S(1)}, f32[128,128]{1,0:T(8,128)S(1)}) custom-call(f32[8,48,128]{2,1,0:T(8,128)S(1)} %all_to_all.29.blocks_ref, s32[1,256]{1,0:T(1,128)S(1)} %get-tuple-element.5.order_ref), custom_call_target="tpu_custom_call" | custom-call | flops 5000000000 | bytes 400000 | tf_op jit(solution)/shard_map/cond/branch_1_fun/turn_pair/pallas_call | solution.py:148
  81.1 0.0 collective-permute-done
  81.1 0.0 copy-start.1
  81.1 0.0 collective-permute-done.5
  81.1 0.0 collective-permute-done.6
  81.2 0.0 collective-permute-done.7
  81.2 0.0 collective-permute-done.2
  81.2 0.0 copy-start.3
  81.2 0.7 copy-done.3
  81.9 0.0 copy-start.4
  81.9 0.7 fusion.6
  82.6 0.2 copy-done.4
  82.9 1.1 maximum_select_fusion
  84.0 0.0 copy-done.1
  84.0 1.0 fusion.1
  85.0 0.7 pad_maximum_fusion.3
  85.8 3.4 %all-to-all-start.3 = ((f32[8,80,128]{2,1,0:T(8,128)}), f32[8,80,128]{2,1,0:T(8,128)S(1)}, u32[]{:S(2)}, u32[]{:S(2)}) async-start(f32[8,80,128]{2,1,0:T(8,128)} %pad_maximum_fusion.3), calls=%async_computation.3 | async-start | bytes 655360 | tf_op jit(solution)/shard_map/all_to_all | solution.py:244
  89.2 0.2 copy.5
  89.4 8.0 %all-to-all-done.3 = f32[8,80,128]{2,1,0:T(8,128)S(1)} async-done(((f32[8,80,128]{2,1,0:T(8,128)}), f32[8,80,128]{2,1,0:T(8,128)S(1)}, u32[]{:S(2)}, u32[]{:S(2)}) %all-to-all-start.3) | async-done | bytes 327712 | tf_op jit(solution)/shard_map/all_to_all | solution.py:244
  97.4 0.7 broadcast_in_dim.22
  98.0 8.8 %all-to-all-start.4 = ((f32[8,32,128]{2,1,0:T(8,128)}), f32[8,32,128]{2,1,0:T(8,128)S(1)}, u32[]{:S(2)}, u32[]{:S(2)}) async-start(f32[8,32,128]{2,1,0:T(8,128)} %broadcast_in_dim.22), calls=%async_computation.4 | async-start | bytes 262144 | tf_op jit(solution)/shard_map/all_to_all | solution.py:54
  106.9 4.5 %turn_pair.3 = (f32[256,128]{1,0:T(8,128)S(1)}, f32[128,128]{1,0:T(8,128)S(1)}) custom-call(f32[8,48,128]{2,1,0:T(8,128)S(1)} %slice.42.blocks_ref, s32[1,256]{1,0:T(1,128)S(1)} %bitcast.15), custom_call_target="tpu_custom_call" | custom-call | flops 5000000000 | bytes 400000 | tf_op jit(solution)/shard_map/turn_pair/pallas_call | solution.py:148
  111.4 0.0 copy-start.2
  111.5 7.0 %all-to-all-done.4 = f32[8,32,128]{2,1,0:T(8,128)S(1)} async-done(((f32[8,32,128]{2,1,0:T(8,128)}), f32[8,32,128]{2,1,0:T(8,128)S(1)}, u32[]{:S(2)}, u32[]{:S(2)}) %all-to-all-start.4) | async-done | bytes 131104 | tf_op jit(solution)/shard_map/all_to_all | solution.py:54
  118.4 0.7 broadcast_in_dim.23
  119.1 3.6 %all-to-all-start.5 = ((f32[8,32,128]{2,1,0:T(8,128)}), f32[8,32,128]{2,1,0:T(8,128)S(1)}, u32[]{:S(2)}, u32[]{:S(2)}) async-start(f32[8,32,128]{2,1,0:T(8,128)} %broadcast_in_dim.23), calls=%async_computation.5 | async-start | bytes 262144 | tf_op jit(solution)/shard_map/all_to_all | solution.py:54
  122.6 0.0 copy-done.2
  122.7 0.6 fusion.given_ref
  123.2 5.3 %all-to-all-done.5.cross_ref = f32[8,32,128]{2,1,0:T(8,128)S(1)} async-done(((f32[8,32,128]{2,1,0:T(8,128)}), f32[8,32,128]{2,1,0:T(8,128)S(1)}, u32[]{:S(2)}, u32[]{:S(2)}) %all-to-all-start.5) | async-done | bytes 131104 | tf_op jit(solution)/shard_map/all_to_all | solution.py:54
  128.5 6.2 %sweep_last.1 = (f32[1024,256]{1,0:T(8,128)}, f32[1,256]{1,0:T(1,128)}) custom-call(f32[8,32,128]{2,1,0:T(8,128)S(1)} %all-to-all-done.5.cross_ref, f32[128,128]{1,0:T(8,128)S(1)} %get-tuple-element.45.gram_ref, f32[256,128]{1,0:T(8,128)S(1)} %get-tuple-element.46.given_basis_ref, f32[128,128]{1,0:T(8,128)S(1)} %get-tuple-element.47.given_gram_ref, ...), custom_call_target="tpu_custom_call" | custom-call | tf_op jit(solution)/shard_map/sweep_last/pallas_call | solution.py:182
  (17 shorter events, 0.2 us)
Async XLA Ops:
  0.6 2.7 %copy-start = (f32[1024,256]{1,0:T(8,128)S(1)}, f32[1024,256]{1,0:T(8,128)}, u32[]{:S(2)}) copy-start(f32[1024,256]{1,0:T(8,128)} %param.4) | copy-start | bytes 3145732
  4.1 14.0 %collective-permute-start.3 = (f32[264,256]{1,0:T(8,128)S(1)}, f32[264,256]{1,0:T(8,128)}, u32[]{:S(2)}, u32[]{:S(2)}) collective-permute-start(f32[264,256]{1,0:T(8,128)S(1)} %get-tuple-element.29), channel_id=1, source_target_pairs={{192,128},{448,384},{193,129},{449,385},{194,130},{450,386},{195,1... | collective-permute-start | bytes 811016 | tf_op jit(solution)/shard_map/ppermute | solution.py:26
  5.3 12.7 %collective-permute-start.4 = (f32[264,256]{1,0:T(8,128)S(1)}, f32[264,256]{1,0:T(8,128)}, u32[]{:S(2)}, u32[]{:S(2)}) collective-permute-start(f32[264,256]{1,0:T(8,128)S(1)} %get-tuple-element.30), channel_id=1, source_target_pairs={{192,64},{448,320},{193,65},{449,321},{194,66},{450,322},{195,67},... | collective-permute-start | bytes 811016 | tf_op jit(solution)/shard_map/ppermute | solution.py:26
  6.7 11.3 %all-to-all-start.1 = ((f32[8,48,128]{2,1,0:T(8,128)}), f32[8,48,128]{2,1,0:T(8,128)S(1)}, u32[]{:S(2)}, u32[]{:S(2)}) async-start(f32[8,48,128]{2,1,0:T(8,128)} %bitcast), calls=%async_computation.1 | async-start | bytes 393216 | tf_op jit(solution)/shard_map/all_to_all | solution.py:60
  11.2 36.6 %collective-permute-start.1 = (f32[752,256]{1,0:T(8,128)S(1)}, f32[752,256]{1,0:T(8,128)S(1)}, u32[]{:S(2)}, u32[]{:S(2)}) collective-permute-start(f32[752,256]{1,0:T(8,128)S(1)} %slice.29), channel_id=1, source_target_pairs={{0,64},{256,320},{64,128},{320,384},{128,192},{384,448},{192,0},{4... | collective-permute-start | bytes 2310152 | tf_op jit(solution)/shard_map/ppermute | solution.py:26
  18.7 29.9 %all-to-all-start.2 = ((f32[8,48,128]{2,1,0:T(8,128)}), f32[8,48,128]{2,1,0:T(8,128)S(1)}, u32[]{:S(2)}, u32[]{:S(2)}) async-start(f32[8,48,128]{2,1,0:T(8,128)} %broadcast_in_dim.18), calls=%async_computation.2 | async-start | bytes 393216 | tf_op jit(solution)/shard_map/all_to_all | solution.py:54
  31.3 17.3 %copy-start.5 = (s32[1,256]{1,0:T(1,128)S(1)}, s32[1,256]{1,0:T(1,128)}, u32[]{:S(2)}) copy-start(s32[1,256]{1,0:T(1,128)} %param.5) | copy-start | bytes 3076
  31.3 49.8 %collective-permute-start = (f32[272,256]{1,0:T(8,128)S(1)}, f32[272,256]{1,0:T(8,128)S(1)}, u32[]{:S(2)}, u32[]{:S(2)}) collective-permute-start(f32[272,256]{1,0:T(8,128)S(1)} %split.9), channel_id=1, source_target_pairs={{0,64},{64,128},{128,192},{192,256},{256,320},{320,384},{384,448},... | collective-permute-start | bytes 835592 | tf_op jit(solution)/shard_map/ppermute | solution.py:26
  37.2 43.9 %collective-permute-start.5 = (f32[264,256]{1,0:T(8,128)}, f32[264,256]{1,0:T(8,128)}, u32[]{:S(2)}, u32[]{:S(2)}) collective-permute-start(f32[264,256]{1,0:T(8,128)} %collective-permute-done.3), channel_id=1, source_target_pairs={{128,256},{384,0},{129,257},{385,1},{130,258},{386,2},{131,259},{3... | collective-permute-start | bytes 811016 | tf_op jit(solution)/shard_map/ppermute | solution.py:26
  46.5 34.6 %collective-permute-start.6 = (f32[264,256]{1,0:T(8,128)}, f32[264,256]{1,0:T(8,128)}, u32[]{:S(2)}, u32[]{:S(2)}) collective-permute-start(f32[264,256]{1,0:T(8,128)} %collective-permute-done.4), channel_id=1, source_target_pairs={{64,256},{320,0},{65,257},{321,1},{66,258},{322,2},{67,259},{323,3... | collective-permute-start | bytes 811016 | tf_op jit(solution)/shard_map/ppermute | solution.py:26
  47.9 33.3 %collective-permute-start.2 = (f32[224,256]{1,0:T(8,128)S(1)}, f32[224,256]{1,0:T(8,128)S(1)}, u32[]{:S(2)}, u32[]{:S(2)}) collective-permute-start(f32[224,256]{1,0:T(8,128)S(1)} %slice.38), channel_id=1, source_target_pairs={{0,256},{256,0},{1,257},{257,1},{2,258},{258,2},{3,259},{259,3},{4... | collective-permute-start | bytes 688136 | tf_op jit(solution)/shard_map/ppermute | solution.py:26
  48.7 32.5 %collective-permute-start.7 = (f32[56,128]{1,0:T(8,128)S(1)}, f32[56,128]{1,0:T(8,128)S(1)}, u32[]{:S(2)}, u32[]{:S(2)}) collective-permute-start(f32[56,128]{1,0:T(8,128)S(1)} %pad_maximum_fusion.5), channel_id=1, source_target_pairs={{0,64},{64,128},{128,192},{192,256},{256,320},{320,384},{384,448},... | collective-permute-start | bytes 86024 | tf_op jit(solution)/shard_map/ppermute | solution.py:26
  81.1 2.9 %copy-start.1 = (f32[272,256]{1,0:T(8,128)}, f32[272,256]{1,0:T(8,128)S(1)}, u32[]{:S(2)}) copy-start(f32[272,256]{1,0:T(8,128)S(1)} %collective-permute-done) | copy-start | bytes 835588
  81.2 0.7 copy-start.3
  81.9 0.9 copy-start.4
  85.8 11.6 %all-to-all-start.3 = ((f32[8,80,128]{2,1,0:T(8,128)}), f32[8,80,128]{2,1,0:T(8,128)S(1)}, u32[]{:S(2)}, u32[]{:S(2)}) async-start(f32[8,80,128]{2,1,0:T(8,128)} %pad_maximum_fusion.3), calls=%async_computation.3 | async-start | bytes 655360 | tf_op jit(solution)/shard_map/all_to_all | solution.py:244
  98.0 20.4 %all-to-all-start.4 = ((f32[8,32,128]{2,1,0:T(8,128)}), f32[8,32,128]{2,1,0:T(8,128)S(1)}, u32[]{:S(2)}, u32[]{:S(2)}) async-start(f32[8,32,128]{2,1,0:T(8,128)} %broadcast_in_dim.22), calls=%async_computation.4 | async-start | bytes 262144 | tf_op jit(solution)/shard_map/all_to_all | solution.py:54
  111.4 11.2 %copy-start.2 = (f32[272,256]{1,0:T(8,128)S(1)}, f32[272,256]{1,0:T(8,128)}, u32[]{:S(2)}) copy-start(f32[272,256]{1,0:T(8,128)} %copy-done.1) | copy-start | bytes 835588
  119.1 9.4 %all-to-all-start.5 = ((f32[8,32,128]{2,1,0:T(8,128)}), f32[8,32,128]{2,1,0:T(8,128)S(1)}, u32[]{:S(2)}, u32[]{:S(2)}) async-start(f32[8,32,128]{2,1,0:T(8,128)} %broadcast_in_dim.23), calls=%async_computation.5 | async-start | bytes 262144 | tf_op jit(solution)/shard_map/all_to_all | solution.py:54

commit v7 on v6

--- a/solution.py
+++ b/solution.py
@@ -128,33 +128,46 @@
     )
 
 
-def picked(blocks, order, first):
-    half = blocks.shape[1]
-    gram = whole_gram(blocks[:half], blocks[half : 2 * half], blocks[2 * half :])
-    basis, moved = swept(gram, True)
+def pair_gram(blocks_ref):
+    half = blocks_ref.shape[2]
+    blocks = blocks_ref[...].reshape(3 * half, half)
+    return whole_gram(blocks[:half], blocks[half : 2 * half], blocks[2 * half :])
+
+
+def turn_kernel(first, blocks_ref, order_ref, basis_ref):
+    half = blocks_ref.shape[2]
+    basis, _ = swept(pair_gram(blocks_ref), False)
     down = lax.broadcasted_iota(jnp.int32, (2 * half, half), 0)
-    chosen = jnp.where(down == order[:, first : first + half], 1.0, 0.0).astype(jnp.bfloat16)
-    columns = halves(picks(halves(moved), chosen))
-    return picks(halves(basis), chosen), picks(columns, chosen, DOWN)
-
-
-def turn_kernel(first, blocks_ref, order_ref, basis_ref, gram_ref):
-    half = blocks_ref.shape[2]
-    basis_ref[...], gram_ref[...] = picked(blocks_ref[...].reshape(3 * half, half), order_ref[...], first)
+    chosen = jnp.where(down == order_ref[:, first : first + half], 1.0, 0.0).astype(jnp.bfloat16)
+    basis_ref[...] = picks(halves(basis), chosen)
 
 
 def turn_pair(blocks, order, first):
     half = blocks.shape[2]
     return pl.pallas_call(
         functools.partial(turn_kernel, first),
-        out_shape=(
-            jax.ShapeDtypeStruct((2 * half, half), jnp.float32),
-            jax.ShapeDtypeStruct((half, half), jnp.float32),
-        ),
+        out_shape=jax.ShapeDtypeStruct((2 * half, half), jnp.float32),
         compiler_params=pltpu.CompilerParams(vmem_limit_bytes=40 * 2**20),
         cost_estimate=pl.CostEstimate(flops=5 * 10**9, bytes_accessed=4 * 10**5, transcendentals=0),
         name="turn_pair",
     )(blocks, order)
+
+
+def gram_kernel(own_ref, kept_ref, behind_ref, given_ref, own_out_ref, behind_out_ref):
+    for blocks_ref, basis_ref, out_ref in ((own_ref, kept_ref, own_out_ref), (behind_ref, given_ref, behind_out_ref)):
+        basis = halves(basis_ref[...])
+        out_ref[...] = times(basis, halves(times(halves(pair_gram(blocks_ref)), basis)), DOWN)
+
+
+def turned_grams(own, kept, behind, given):
+    half = kept.shape[1]
+    return pl.pallas_call(
+        gram_kernel,
+        out_shape=(jax.ShapeDtypeStruct((half, half), jnp.float32),) * 2,
+        compiler_params=pltpu.CompilerParams(vmem_limit_bytes=40 * 2**20),
+        cost_estimate=pl.CostEstimate(flops=10**9, bytes_accessed=8 * 10**5, transcendentals=0),
+        name="turned_grams",
+    )(own, kept, behind, given)
 
 
 def last_kernel(rows, cross_ref, gram_ref, given_basis_ref, given_gram_ref, kept_ref, given_ref,
@@ -221,12 +234,13 @@
     arrived = send(jnp.concatenate([slices, order], axis=0), [(i, (i + 1) % 8) for i in range(8)])
 
     def turn_first(slices, keep):
-        return turn_pair(spread(slices, NEAR), keep, 0)
-
-    kept_basis, kept_gram = lax.cond(
+        blocks = spread(slices, NEAR)
+        return turn_pair(blocks, keep, 0), blocks
+
+    kept_basis, own_blocks = lax.cond(
         keep[0, 0] >= 0,
         turn_first,
-        lambda *_: (jnp.zeros((width, half), jnp.float32), jnp.zeros((half, half), jnp.float32)),
+        lambda *_: (jnp.zeros((width, half), jnp.float32), jnp.zeros((8, share, half), jnp.float32)),
         slices,
         keep,
     )
@@ -244,8 +258,12 @@
     parts = lax.all_to_all(jnp.concatenate(parts, axis=1), NEAR, 0, 0, tiled=True)
     cross = far_sum(jnp.sum(parts[:, :cut], axis=0))
     behind_keep = arrived[share : share + 2].reshape(1, width).astype(jnp.int32)
-    given_basis, given_gram = turn_pair(parts[:, cut:], behind_keep, half)
-    cross, given_basis, given_gram = lax.optimization_barrier((cross, given_basis, given_gram))
+    behind_blocks = parts[:, cut:]
+    given_basis = turn_pair(behind_blocks, behind_keep, half)
+    kept_gram, given_gram = turned_grams(own_blocks, kept_basis, behind_blocks, given_basis)
+    cross, given_basis, kept_gram, given_gram = lax.optimization_barrier(
+        (cross, given_basis, kept_gram, given_gram)
+    )
     rotated, norms = sweep_last(
         rows * lax.axis_size(ROW),
         spread(cross, NEAR),

time: 136 us -> 136 us (level)
  Pallas kernels: 15.3 us -> 16.8 us
    pallas_call x2 -> x3, Pallas kernels: 9.07 us -> 10.6 us  [the longest x2 8.79 us: turn_pair(): pl.pallas_call(functools.partial(turn_kernel, first), out_shape=jax.Shape...]
  transfers between devices with their start and end apart: 13 -> 13, of which waited for: 4 -> 4; matrix products, arithmetic and copies ran while one was open for 2% -> 2% of each run, Pallas kernels for 7% -> 8%
where the time goes in v7:
time: 136 us; the launch traced here: 135 us
  starting transfers between devices  75.5 us (56%)
  waiting for transfers between devices  19.9 us (15%)
  Pallas kernels  16.8 us (12%)
  blocking collectives  9.91 us (7%)
  matrix products  4.88 us (4%)
  local copies, waits for them, and re-layouts  3.92 us (3%)
  other arithmetic  2.64 us (2%)
  between operations  1.67 us (1%)
    ppermute x8, starting transfers between devices, send(): return lax.ppermute(shard, COL, pairs)  43.2 us
    all_to_all x3, starting transfers between devices, spread(): return lax.all_to_all(copies, axis, 0, 0, tiled=True)  24.4 us
    all_to_all x3, waiting for transfers between devices, spread(): return lax.all_to_all(copies, axis, 0, 0, tiled=True)  11 us
    all_to_all x1, blocking collectives, spread(): return lax.all_to_all(copies, axis, 0, 0, tiled=True)  9.91 us
    pallas_call x2, Pallas kernels, turn_pair(): pl.pallas_call(functools.partial(turn_kernel, first), out_shape=jax.Shape...  8.79 us
    all_to_all x1, waiting for transfers between devices, shards(): lax.all_to_all(jnp.concatenate(parts, axis=1), NEAR, 0, 0, tiled=True)  7.95 us
    pallas_call x1, Pallas kernels, sweep_last(): pl.pallas_call(functools.partial(last_kernel, rows), grid=(kept.shape[0]...  6.21 us
    all_to_all x1, starting transfers between devices, near_sum(): return jnp.sum(lax.all_to_all(slices, NEAR, 0, 0, tiled=True), axis=0)  4.47 us
  transfers between devices with their start and end apart: 13, of which 4 were waited for; matrix products, arithmetic and copies ran while one was open for 2% of the time, Pallas kernels for 8%

profile of v7, /device:TPU:4, one launch (start us, length us, event | category | flops | bytes accessed | tf_op | source)
XLA Modules:
  0.0 135.2 jit_solution(3073582515564568326)
XLA Ops:
  0.6 0.0 copy-start
  0.6 2.6 %fusion.5 = f32[256,256]{1,0:T(8,128)S(1)} fusion(f32[1024,256]{1,0:T(8,128)} %param.4), kind=kOutput, calls=%fused_computation.12 | convolution fusion | flops 402653184 | bytes 1310720 | tf_op jit(solution)/shard_map/dot_general | solution.py:42
  3.3 0.0 copy-done
  3.4 0.7 pad_maximum_fusion.4
  4.0 1.3 collective-permute-start.3
  5.3 1.4 %collective-permute-start.4 = (f32[264,256]{1,0:T(8,128)S(1)}, f32[264,256]{1,0:T(8,128)}, u32[]{:S(2)}, u32[]{:S(2)}) collective-permute-start(f32[264,256]{1,0:T(8,128)S(1)} %get-tuple-element.31), channel_id=1, source_target_pairs={{192,64},{448,320},{193,65},{449,321},{194,66},{450,322},{195,67},... | collective-permute-start | bytes 811016 | tf_op jit(solution)/shard_map/ppermute | solution.py:26
  6.7 4.5 %all-to-all-start.1 = ((f32[8,48,128]{2,1,0:T(8,128)}), f32[8,48,128]{2,1,0:T(8,128)S(1)}, u32[]{:S(2)}, u32[]{:S(2)}) async-start(f32[8,48,128]{2,1,0:T(8,128)} %bitcast), calls=%async_computation.1 | async-start | bytes 393216 | tf_op jit(solution)/shard_map/all_to_all | solution.py:60
  11.2 0.1 slice.29
  11.2 5.9 %collective-permute-start.1 = (f32[752,256]{1,0:T(8,128)S(1)}, f32[752,256]{1,0:T(8,128)S(1)}, u32[]{:S(2)}, u32[]{:S(2)}) collective-permute-start(f32[752,256]{1,0:T(8,128)S(1)} %slice.29), channel_id=1, source_target_pairs={{0,64},{256,320},{64,128},{320,384},{128,192},{384,448},{192,0},{4... | collective-permute-start | bytes 2310152 | tf_op jit(solution)/shard_map/ppermute | solution.py:26
  17.1 0.9 all-to-all-done.1
  18.0 0.0 collective-permute-done.3
  18.1 0.0 collective-permute-done.4
  18.1 0.7 broadcast_in_dim.18
  18.8 12.5 %all-to-all-start.2 = ((f32[8,48,128]{2,1,0:T(8,128)}), f32[8,48,128]{2,1,0:T(8,128)S(1)}, u32[]{:S(2)}, u32[]{:S(2)}) async-start(f32[8,48,128]{2,1,0:T(8,128)} %broadcast_in_dim.18), calls=%async_computation.2 | async-start | bytes 393216 | tf_op jit(solution)/shard_map/all_to_all | solution.py:54
  31.3 0.0 copy-start.7
  31.3 5.9 %collective-permute-start = (f32[272,256]{1,0:T(8,128)S(1)}, f32[272,256]{1,0:T(8,128)S(1)}, u32[]{:S(2)}, u32[]{:S(2)}) collective-permute-start(f32[272,256]{1,0:T(8,128)S(1)} %split.9), channel_id=1, source_target_pairs={{0,64},{64,128},{128,192},{192,256},{256,320},{320,384},{384,448},... | collective-permute-start | bytes 835592 | tf_op jit(solution)/shard_map/ppermute | solution.py:26
  37.2 9.3 %collective-permute-start.5 = (f32[264,256]{1,0:T(8,128)}, f32[264,256]{1,0:T(8,128)}, u32[]{:S(2)}, u32[]{:S(2)}) collective-permute-start(f32[264,256]{1,0:T(8,128)} %collective-permute-done.3), channel_id=1, source_target_pairs={{128,256},{384,0},{129,257},{385,1},{130,258},{386,2},{131,259},{3... | collective-permute-start | bytes 811016 | tf_op jit(solution)/shard_map/ppermute | solution.py:26
  46.5 1.4 %collective-permute-start.6 = (f32[264,256]{1,0:T(8,128)}, f32[264,256]{1,0:T(8,128)}, u32[]{:S(2)}, u32[]{:S(2)}) collective-permute-start(f32[264,256]{1,0:T(8,128)} %collective-permute-done.4), channel_id=1, source_target_pairs={{64,256},{320,0},{65,257},{321,1},{66,258},{322,2},{67,259},{323,3... | collective-permute-start | bytes 811016 | tf_op jit(solution)/shard_map/ppermute | solution.py:26
  47.9 0.0 collective-permute-done.1
  47.9 0.7 collective-permute-start.2
  48.6 0.0 copy-done.7
  48.6 0.0 all-to-all-done.2
  48.6 17.5 %collective-permute-start.7 = (f32[56,128]{1,0:T(8,128)S(1)}, f32[56,128]{1,0:T(8,128)S(1)}, u32[]{:S(2)}, u32[]{:S(2)}) collective-permute-start(f32[56,128]{1,0:T(8,128)S(1)} %pad_maximum_fusion.5), channel_id=1, source_target_pairs={{0,64},{64,128},{128,192},{192,256},{256,320},{320,384},{384,448},... | collective-permute-start | bytes 86024 | tf_op jit(solution)/shard_map/ppermute | solution.py:26
  66.1 0.5 slice.33
  67.3 14.8 %conditional.1 = (f32[256,128]{1,0:T(8,128)S(1)}, f32[8,48,128]{2,1,0:T(8,128)}) conditional(s32[]{:T(128)} %bitcast.3, () %tuple.22, (f32[48,128]{1,0:T(8,128)S(1)}, s32[1,256]{1,0:T(1,128)S(1)}) %tuple.30), branch_computations={%region_2.0_spmd, %region_3.0_spmd} | conditional | flops 5000000000 | bytes 1014416 | solution.py:240
  67.3 9.9 %all_to_all.29.blocks_ref = f32[8,48,128]{2,1,0:T(8,128)} all-to-all(f32[8,48,128]{2,1,0:T(8,128)S(1)} %broadcast_in_dim.3), channel_id=1, replica_groups=mesh['z_hi'=2,'x'=4,'z_lo'=8,'y'=4,'core'=2] {'y','core'}, dimensions={0} | all-to-all | bytes 393216 | tf_op jit(solution)/shard_map/cond/branch_1_fun/all_to_all | solution.py:54
  77.2 4.9 %turn_pair.2 = f32[256,128]{1,0:T(8,128)S(1)} custom-call(f32[8,48,128]{2,1,0:T(8,128)} %all_to_all.29.blocks_ref, s32[1,256]{1,0:T(1,128)S(1)} %get-tuple-element.5.order_ref), custom_call_target="tpu_custom_call" | custom-call | flops 5000000000 | bytes 400000 | tf_op jit(solution)/shard_map/cond/branch_1_fun/turn_pair/pallas_call | solution.py:147
  82.1 0.0 copy-start.3
  82.1 0.0 collective-permute-done
  82.1 0.0 copy-start.1
  82.1 0.0 collective-permute-done.5
  82.2 0.0 collective-permute-done.6
  82.2 0.0 collective-permute-done.7
  82.2 0.0 collective-permute-done.2
  82.2 0.0 copy-start.5
  82.2 0.7 copy-done.5
  82.9 0.0 copy-done.3
  82.9 0.0 copy-start.6
  82.9 0.7 fusion.6
  83.6 0.2 copy-done.6
  83.9 1.1 maximum_select_fusion
  85.0 0.0 copy-done.1
  85.0 1.0 fusion.1
  86.0 0.7 pad_maximum_fusion.3
  86.8 3.4 %all-to-all-start.3 = ((f32[8,80,128]{2,1,0:T(8,128)}), f32[8,80,128]{2,1,0:T(8,128)S(1)}, u32[]{:S(2)}, u32[]{:S(2)}) async-start(f32[8,80,128]{2,1,0:T(8,128)} %pad_maximum_fusion.3), calls=%async_computation.3 | async-start | bytes 655360 | tf_op jit(solution)/shard_map/all_to_all | solution.py:258
  90.2 0.2 copy.5
  90.4 8.0 %all-to-all-done.3 = f32[8,80,128]{2,1,0:T(8,128)S(1)} async-done(((f32[8,80,128]{2,1,0:T(8,128)}), f32[8,80,128]{2,1,0:T(8,128)S(1)}, u32[]{:S(2)}, u32[]{:S(2)}) %all-to-all-start.3) | async-done | bytes 327712 | tf_op jit(solution)/shard_map/all_to_all | solution.py:258
  98.4 0.7 broadcast_in_dim.22
  99.1 8.3 %all-to-all-start.4 = ((f32[8,32,128]{2,1,0:T(8,128)}), f32[8,32,128]{2,1,0:T(8,128)S(1)}, u32[]{:S(2)}, u32[]{:S(2)}) async-start(f32[8,32,128]{2,1,0:T(8,128)} %broadcast_in_dim.22), calls=%async_computation.4 | async-start | bytes 262144 | tf_op jit(solution)/shard_map/all_to_all | solution.py:54
  107.4 0.0 copy-start.4
  107.4 3.9 %turn_pair.3.given_ref.given_basis_ref = f32[256,128]{1,0:T(8,128)S(1)} custom-call(f32[8,48,128]{2,1,0:T(8,128)S(1)} %slice.42.blocks_ref.behind_ref, s32[1,256]{1,0:T(1,128)S(1)} %bitcast.15), custom_call_target="tpu_custom_call" | custom-call | flops 5000000000 | bytes 400000 | tf_op jit(solution)/shard_map/turn_pair/pallas_call | solution.py:147
  111.3 0.0 copy-done.4
  111.3 1.8 %turned_grams.1 = (f32[128,128]{1,0:T(8,128)S(1)}, f32[128,128]{1,0:T(8,128)S(1)}) custom-call(f32[8,48,128]{2,1,0:T(8,128)} %get-tuple-element.43.own_ref, f32[256,128]{1,0:T(8,128)S(1)} %copy-done.4, f32[8,48,128]{2,1,0:T(8,128)S(1)} %slice.42.blocks_ref.behind_ref, f32[256,128]{1,0:T(8,128)S(1)} %turn_pair.3.given_ref.given_basis_ref), custom_call_target="tpu_custom_call" | custom-call | flops 1000000000 | bytes 800000 | tf_op jit(solution)/shard_map/turned_grams/pallas_call | solution.py:164
  113.1 0.0 copy-start.2
  113.1 5.7 %all-to-all-done.4 = f32[8,32,128]{2,1,0:T(8,128)S(1)} async-done(((f32[8,32,128]{2,1,0:T(8,128)}), f32[8,32,128]{2,1,0:T(8,128)S(1)}, u32[]{:S(2)}, u32[]{:S(2)}) %all-to-all-start.4) | async-done | bytes 131104 | tf_op jit(solution)/shard_map/all_to_all | solution.py:54
  118.9 0.7 broadcast_in_dim.23
  119.6 3.6 %all-to-all-start.5 = ((f32[8,32,128]{2,1,0:T(8,128)}), f32[8,32,128]{2,1,0:T(8,128)S(1)}, u32[]{:S(2)}, u32[]{:S(2)}) async-start(f32[8,32,128]{2,1,0:T(8,128)} %broadcast_in_dim.23), calls=%async_computation.5 | async-start | bytes 262144 | tf_op jit(solution)/shard_map/all_to_all | solution.py:54
  123.1 0.0 copy-done.2
  123.1 0.6 fusion.given_ref
  123.7 5.3 %all-to-all-done.5.cross_ref = f32[8,32,128]{2,1,0:T(8,128)S(1)} async-done(((f32[8,32,128]{2,1,0:T(8,128)}), f32[8,32,128]{2,1,0:T(8,128)S(1)}, u32[]{:S(2)}, u32[]{:S(2)}) %all-to-all-start.5) | async-done | bytes 131104 | tf_op jit(solution)/shard_map/all_to_all | solution.py:54
  129.0 6.2 %sweep_last.1 = (f32[1024,256]{1,0:T(8,128)}, f32[1,256]{1,0:T(1,128)}) custom-call(f32[8,32,128]{2,1,0:T(8,128)S(1)} %all-to-all-done.5.cross_ref, f32[128,128]{1,0:T(8,128)S(1)} %get-tuple-element.47.gram_ref, f32[256,128]{1,0:T(8,128)S(1)} %turn_pair.3.given_ref.given_basis_ref, f32[128,128]{1,0:T(8,128)S(1)} %get-tuple-element.49.given_gram_ref, ...), custom_call_target="tpu_custom_call" | custom-call | tf_op jit(solution)/shard_map/sweep_last/pallas_call | solution.py:195
  (17 shorter events, 0.2 us)
Async XLA Ops:
  0.6 2.7 %copy-start = (f32[1024,256]{1,0:T(8,128)S(1)}, f32[1024,256]{1,0:T(8,128)}, u32[]{:S(2)}) copy-start(f32[1024,256]{1,0:T(8,128)} %param.4) | copy-start | bytes 3145732
  4.0 14.0 %collective-permute-start.3 = (f32[264,256]{1,0:T(8,128)S(1)}, f32[264,256]{1,0:T(8,128)}, u32[]{:S(2)}, u32[]{:S(2)}) collective-permute-start(f32[264,256]{1,0:T(8,128)S(1)} %get-tuple-element.30), channel_id=1, source_target_pairs={{192,128},{448,384},{193,129},{449,385},{194,130},{450,386},{195,1... | collective-permute-start | bytes 811016 | tf_op jit(solution)/shard_map/ppermute | solution.py:26
  5.3 12.7 %collective-permute-start.4 = (f32[264,256]{1,0:T(8,128)S(1)}, f32[264,256]{1,0:T(8,128)}, u32[]{:S(2)}, u32[]{:S(2)}) collective-permute-start(f32[264,256]{1,0:T(8,128)S(1)} %get-tuple-element.31), channel_id=1, source_target_pairs={{192,64},{448,320},{193,65},{449,321},{194,66},{450,322},{195,67},... | collective-permute-start | bytes 811016 | tf_op jit(solution)/shard_map/ppermute | solution.py:26
  6.7 11.3 %all-to-all-start.1 = ((f32[8,48,128]{2,1,0:T(8,128)}), f32[8,48,128]{2,1,0:T(8,128)S(1)}, u32[]{:S(2)}, u32[]{:S(2)}) async-start(f32[8,48,128]{2,1,0:T(8,128)} %bitcast), calls=%async_computation.1 | async-start | bytes 393216 | tf_op jit(solution)/shard_map/all_to_all | solution.py:60
  11.2 36.6 %collective-permute-start.1 = (f32[752,256]{1,0:T(8,128)S(1)}, f32[752,256]{1,0:T(8,128)S(1)}, u32[]{:S(2)}, u32[]{:S(2)}) collective-permute-start(f32[752,256]{1,0:T(8,128)S(1)} %slice.29), channel_id=1, source_target_pairs={{0,64},{256,320},{64,128},{320,384},{128,192},{384,448},{192,0},{4... | collective-permute-start | bytes 2310152 | tf_op jit(solution)/shard_map/ppermute | solution.py:26
  18.8 29.8 %all-to-all-start.2 = ((f32[8,48,128]{2,1,0:T(8,128)}), f32[8,48,128]{2,1,0:T(8,128)S(1)}, u32[]{:S(2)}, u32[]{:S(2)}) async-start(f32[8,48,128]{2,1,0:T(8,128)} %broadcast_in_dim.18), calls=%async_computation.2 | async-start | bytes 393216 | tf_op jit(solution)/shard_map/all_to_all | solution.py:54
  31.3 17.3 %copy-start.7 = (s32[1,256]{1,0:T(1,128)S(1)}, s32[1,256]{1,0:T(1,128)}, u32[]{:S(2)}) copy-start(s32[1,256]{1,0:T(1,128)} %param.5) | copy-start | bytes 3076
  31.3 50.8 %collective-permute-start = (f32[272,256]{1,0:T(8,128)S(1)}, f32[272,256]{1,0:T(8,128)S(1)}, u32[]{:S(2)}, u32[]{:S(2)}) collective-permute-start(f32[272,256]{1,0:T(8,128)S(1)} %split.9), channel_id=1, source_target_pairs={{0,64},{64,128},{128,192},{192,256},{256,320},{320,384},{384,448},... | collective-permute-start | bytes 835592 | tf_op jit(solution)/shard_map/ppermute | solution.py:26
  37.2 45.0 %collective-permute-start.5 = (f32[264,256]{1,0:T(8,128)}, f32[264,256]{1,0:T(8,128)}, u32[]{:S(2)}, u32[]{:S(2)}) collective-permute-start(f32[264,256]{1,0:T(8,128)} %collective-permute-done.3), channel_id=1, source_target_pairs={{128,256},{384,0},{129,257},{385,1},{130,258},{386,2},{131,259},{3... | collective-permute-start | bytes 811016 | tf_op jit(solution)/shard_map/ppermute | solution.py:26
  46.5 35.7 %collective-permute-start.6 = (f32[264,256]{1,0:T(8,128)}, f32[264,256]{1,0:T(8,128)}, u32[]{:S(2)}, u32[]{:S(2)}) collective-permute-start(f32[264,256]{1,0:T(8,128)} %collective-permute-done.4), channel_id=1, source_target_pairs={{64,256},{320,0},{65,257},{321,1},{66,258},{322,2},{67,259},{323,3... | collective-permute-start | bytes 811016 | tf_op jit(solution)/shard_map/ppermute | solution.py:26
  47.9 34.3 %collective-permute-start.2 = (f32[224,256]{1,0:T(8,128)S(1)}, f32[224,256]{1,0:T(8,128)S(1)}, u32[]{:S(2)}, u32[]{:S(2)}) collective-permute-start(f32[224,256]{1,0:T(8,128)S(1)} %slice.38), channel_id=1, source_target_pairs={{0,256},{256,0},{1,257},{257,1},{2,258},{258,2},{3,259},{259,3},{4... | collective-permute-start | bytes 688136 | tf_op jit(solution)/shard_map/ppermute | solution.py:26
  48.6 33.5 %collective-permute-start.7 = (f32[56,128]{1,0:T(8,128)S(1)}, f32[56,128]{1,0:T(8,128)S(1)}, u32[]{:S(2)}, u32[]{:S(2)}) collective-permute-start(f32[56,128]{1,0:T(8,128)S(1)} %pad_maximum_fusion.5), channel_id=1, source_target_pairs={{0,64},{64,128},{128,192},{192,256},{256,320},{320,384},{384,448},... | collective-permute-start | bytes 86024 | tf_op jit(solution)/shard_map/ppermute | solution.py:26
  82.1 0.8 copy-start.3
  82.1 2.9 %copy-start.1 = (f32[272,256]{1,0:T(8,128)}, f32[272,256]{1,0:T(8,128)S(1)}, u32[]{:S(2)}) copy-start(f32[272,256]{1,0:T(8,128)S(1)} %collective-permute-done) | copy-start | bytes 835588
  82.2 0.8 copy-start.5
  82.9 0.9 copy-start.6
  86.8 11.6 %all-to-all-start.3 = ((f32[8,80,128]{2,1,0:T(8,128)}), f32[8,80,128]{2,1,0:T(8,128)S(1)}, u32[]{:S(2)}, u32[]{:S(2)}) async-start(f32[8,80,128]{2,1,0:T(8,128)} %pad_maximum_fusion.3), calls=%async_computation.3 | async-start | bytes 655360 | tf_op jit(solution)/shard_map/all_to_all | solution.py:258
  99.1 19.8 %all-to-all-start.4 = ((f32[8,32,128]{2,1,0:T(8,128)}), f32[8,32,128]{2,1,0:T(8,128)S(1)}, u32[]{:S(2)}, u32[]{:S(2)}) async-start(f32[8,32,128]{2,1,0:T(8,128)} %broadcast_in_dim.22), calls=%async_computation.4 | async-start | bytes 262144 | tf_op jit(solution)/shard_map/all_to_all | solution.py:54
  107.4 4.0 %copy-start.4 = (f32[256,128]{1,0:T(8,128)S(1)}, f32[256,128]{1,0:T(8,128)}, u32[]{:S(2)}) copy-start(f32[256,128]{1,0:T(8,128)} %copy-done.3) | copy-start | bytes 393220
  113.1 10.0 %copy-start.2 = (f32[272,256]{1,0:T(8,128)S(1)}, f32[272,256]{1,0:T(8,128)}, u32[]{:S(2)}) copy-start(f32[272,256]{1,0:T(8,128)} %copy-done.1) | copy-start | bytes 835588
  119.6 9.4 %all-to-all-start.5 = ((f32[8,32,128]{2,1,0:T(8,128)}), f32[8,32,128]{2,1,0:T(8,128)S(1)}, u32[]{:S(2)}, u32[]{:S(2)}) async-start(f32[8,32,128]{2,1,0:T(8,128)} %broadcast_in_dim.23), calls=%async_computation.5 | async-start | bytes 262144 | tf_op jit(solution)/shard_map/all_to_all | solution.py:54
